TPU v7x, 512 devices: a whole 4x8x8 slice. The times are simulated.
512 devices in a mesh: group: 16 (over y, z_lo), dev: 32 (over z_hi, x, core).
Axes of the slice: x: 4, y: 8, z: 8 (z_hi: 4, z_lo: 2; z = z_hi * 2 + z_lo), core: 2. Of those that a mesh axis runs over, the one named last changes fastest.
Arguments:
- slab: float32 [48, 4194304], P(None, ('group', 'dev'))
- flips: int32 [4194304], P(('group', 'dev')), may hold values 0 or 1
- sampled: int32 [12288], replicated, may hold values from 0 to 4194303, as said below
Outputs:
- mixed: float32 [48, 4194304], P(None, ('group', 'dev'))
- gram: float32 [48, 48], replicated
- factor: float32 [48, 48], replicated
Inputs may be any that keep to these rules, and one draw needn't show every extreme that they name: `sampled`: the indices are distinct and strictly increasing.
All inputs are finite; a program needn't handle non-finite values. No bound on the sum of `flips` on one device may be relied on, other than what follows from the above.
Results may differ from a plain program's by a relative error of at most 0.000098.
Values sent between devices are 32-bit elements; how exact they have to be, the bound alone decides.
No kernel may reach another device: no remote copies, remote signals or barrier semaphores. Data moves between devices by JAX's collectives and lax.ppermute only.
A program may use at most 64 MiB of HBM per device.

v0:
```python
import math

import jax
import jax.numpy as jnp
from jax import lax
from jax.sharding import PartitionSpec as P

SAMPLES = 12288


def from_partner(x, axis, apart):
    return lax.ppermute(x, axis, [(i, i ^ 1 << apart) for i in range(lax.axis_size(axis))])


def walsh_table(length):
    index = jnp.arange(length, dtype=jnp.int32)
    anded = index[:, None] & index[None, :]
    parity = jnp.zeros((length, length), jnp.int32)
    for bit in range(max(length.bit_length() - 1, 0)):
        parity = parity ^ anded >> bit & 1
    return (1 - 2 * parity).astype(jnp.float32)


def per_device(slab, flips, sampled):
    width, rows = slab.shape
    signed = slab * (1 - 2 * flips).astype(jnp.float32)[None, :]
    outer = rows // 128
    blocks = signed.reshape(width, outer, 128)
    blocks = jnp.einsum("cab,db->cad", blocks, walsh_table(128), precision=lax.Precision.HIGHEST)
    blocks = jnp.einsum("cab,da->cdb", blocks, walsh_table(outer), precision=lax.Precision.HIGHEST)
    field = blocks.reshape(width, rows)
    inner_count = lax.axis_size("dev")
    outer_count = lax.axis_size("group")
    inner_rank = lax.axis_index("dev")
    for bit in range(inner_count.bit_length() - 1):
        partner = from_partner(field, "dev", bit)
        upper = inner_rank >> bit & 1 == 1
        field = jnp.where(upper, partner - field, field + partner)
    outer_rank = lax.axis_index("group")
    for bit in range(outer_count.bit_length() - 1):
        partner = from_partner(field, "group", bit)
        upper = outer_rank >> bit & 1 == 1
        field = jnp.where(upper, partner - field, field + partner)
    total_rows = rows * inner_count * outer_count
    mixed = field * jnp.float32(1.0 / math.sqrt(total_rows))
    first_row = (lax.axis_index("group") * inner_count + lax.axis_index("dev")) * rows
    local_index = sampled - first_row
    inside = (local_index >= 0) & (local_index < rows)
    hits = (
        jnp.zeros((rows,), jnp.float32)
        .at[jnp.clip(local_index, 0, rows - 1)]
        .add(inside.astype(jnp.float32))
    )
    partial_gram = jnp.einsum(
        "cr,dr->cd", mixed * hits[None, :], mixed, precision=lax.Precision.HIGHEST
    )
    gram = lax.psum(partial_gram, ("group", "dev")) / jnp.float32(SAMPLES)
    factor = jnp.linalg.cholesky(gram).T
    return (mixed, gram, factor)


def solution(mesh):
    placed = (P(None, ("group", "dev")), P(("group", "dev")), P())
    return jax.shard_map(
        per_device,
        mesh=mesh,
        in_specs=placed,
        out_specs=(P(None, ("group", "dev")), P(), P()),
        check_vma=False,
    )
```

profile of v0, /device:TPU:1, one launch (start us, length us, event | category | flops | bytes accessed | tf_op | source)
XLA Modules:
  0.0 598.3 jit_solution(17510000502997576792)
XLA Ops:
  1.4 1.5 multiply_bitcast_fusion
  3.2 1.4 fusion.3
  4.6 1.5 fusion.31
  7.1 8.8 %collective-permute-start = (f32[48,8192]{1,0:T(8,128)S(1)}, f32[48,8192]{1,0:T(8,128)}, u32[]{:S(2)}, u32[]{:S(2)}) collective-permute-start(f32[48,8192]{1,0:T(8,128)S(1)} %bitcast.28), channel_id=1, source_target_pairs={{0,1},{1,0},{2,3},{3,2},{4,5},{5,4},{6,7},{7,6},{8,9},{9,8},{10,11... | collective-permute-start | bytes 4718600 | tf_op jit(solution)/shard_map/ppermute | solution.py:12
  15.9 3.1 collective-permute-done
  19.0 2.4 add_select_fusion.8
  21.4 1.9 collective-permute-start.1
  23.4 35.7 %collective-permute-done.1 = f32[48,8192]{1,0:T(8,128)} collective-permute-done((f32[48,8192]{1,0:T(8,128)S(1)}, f32[48,8192]{1,0:T(8,128)}, u32[]{:S(2)}, u32[]{:S(2)}) %collective-permute-start.1) | collective-permute-done | bytes 1572896 | tf_op jit(solution)/shard_map/ppermute | solution.py:12
  59.0 1.6 add_select_fusion.7
  60.6 1.9 collective-permute-start.2
  62.6 36.3 %collective-permute-done.2 = f32[48,8192]{1,0:T(8,128)} collective-permute-done((f32[48,8192]{1,0:T(8,128)S(1)}, f32[48,8192]{1,0:T(8,128)}, u32[]{:S(2)}, u32[]{:S(2)}) %collective-permute-start.2) | collective-permute-done | bytes 1572896 | tf_op jit(solution)/shard_map/ppermute | solution.py:12
  98.8 1.6 add_select_fusion.6
  100.4 1.9 collective-permute-start.3
  102.3 68.9 %collective-permute-done.3 = f32[48,8192]{1,0:T(8,128)S(1)} collective-permute-done((f32[48,8192]{1,0:T(8,128)S(1)}, f32[48,8192]{1,0:T(8,128)S(1)}, u32[]{:S(2)}, u32[]{:S(2)}) %collective-permute-start.3) | collective-permute-done | bytes 1572896 | tf_op jit(solution)/shard_map/ppermute | solution.py:12
  171.2 1.6 add_select_fusion.5
  172.8 6.3 %collective-permute-start.4 = (f32[48,8192]{1,0:T(8,128)S(1)}, f32[48,8192]{1,0:T(8,128)}, u32[]{:S(2)}, u32[]{:S(2)}) collective-permute-start(f32[48,8192]{1,0:T(8,128)S(1)} %add_select_fusion.5), channel_id=1, source_target_pairs={{0,16},{1,17},{2,18},{3,19},{4,20},{5,21},{6,22},{7,23},{8,24},{9,... | collective-permute-start | bytes 4718600 | tf_op jit(solution)/shard_map/ppermute | solution.py:12
  179.1 69.1 %collective-permute-done.4 = f32[48,8192]{1,0:T(8,128)} collective-permute-done((f32[48,8192]{1,0:T(8,128)S(1)}, f32[48,8192]{1,0:T(8,128)}, u32[]{:S(2)}, u32[]{:S(2)}) %collective-permute-start.4) | collective-permute-done | bytes 1572896 | tf_op jit(solution)/shard_map/ppermute | solution.py:12
  248.2 1.6 add_select_fusion.4
  249.8 1.9 collective-permute-start.5
  251.7 34.6 %collective-permute-done.5 = f32[48,8192]{1,0:T(8,128)} collective-permute-done((f32[48,8192]{1,0:T(8,128)S(1)}, f32[48,8192]{1,0:T(8,128)}, u32[]{:S(2)}, u32[]{:S(2)}) %collective-permute-start.5) | collective-permute-done | bytes 1572896 | tf_op jit(solution)/shard_map/ppermute | solution.py:12
  286.3 1.6 add_select_fusion.3
  287.9 1.9 collective-permute-start.6
  289.8 33.5 %collective-permute-done.6 = f32[48,8192]{1,0:T(8,128)S(1)} collective-permute-done((f32[48,8192]{1,0:T(8,128)S(1)}, f32[48,8192]{1,0:T(8,128)S(1)}, u32[]{:S(2)}, u32[]{:S(2)}) %collective-permute-start.6) | collective-permute-done | bytes 1572896 | tf_op jit(solution)/shard_map/ppermute | solution.py:12
  323.4 1.6 add_select_fusion.2
  324.9 1.9 collective-permute-start.7
  326.9 71.0 %collective-permute-done.7 = f32[48,8192]{1,0:T(8,128)} collective-permute-done((f32[48,8192]{1,0:T(8,128)S(1)}, f32[48,8192]{1,0:T(8,128)}, u32[]{:S(2)}, u32[]{:S(2)}) %collective-permute-start.7) | collective-permute-done | bytes 1572896 | tf_op jit(solution)/shard_map/ppermute | solution.py:12
  397.8 1.6 add_select_fusion.1
  399.4 4.1 collective-permute-start.8
  403.6 85.2 %scatter_custom_fusion = f32[8192]{0:T(1024)S(1)} fusion(s32[12288]{0:T(1024)S(1)} %compare_select_fusion, f32[12288]{0:T(1024)S(1)} %and_convert_fusion, f32[]{:T(128)} %constant.79.clone.1), kind=kCustom, calls=%fused_computation.86 | custom fusion | flops 12288 | bytes 32772 | tf_op jit(solution)/shard_map/scatter-add | solution.py:52
  490.2 1.6 fusion
  491.9 99.9 %psum.7 = f32[48,48]{0,1:T(8,128)S(1)} all-reduce(f32[48,48]{0,1:T(8,128)S(1)} %fusion), channel_id=1, replica_groups=mesh['group'=16,'dev'=32] {'group','dev'}, use_global_device_ids=true, to_apply=%region_1.2 | all-reduce | flops 2304 | bytes 18432 | tf_op jit(solution)/shard_map/psum | solution.py:57
  591.9 4.4 cholesky.18
  (25 shorter events, 5.4 us)
Async XLA Ops:
  7.1 11.9 %collective-permute-start = (f32[48,8192]{1,0:T(8,128)S(1)}, f32[48,8192]{1,0:T(8,128)}, u32[]{:S(2)}, u32[]{:S(2)}) collective-permute-start(f32[48,8192]{1,0:T(8,128)S(1)} %bitcast.28), channel_id=1, source_target_pairs={{0,1},{1,0},{2,3},{3,2},{4,5},{5,4},{6,7},{7,6},{8,9},{9,8},{10,11... | collective-permute-start | bytes 4718600 | tf_op jit(solution)/shard_map/ppermute | solution.py:12
  21.4 37.6 %collective-permute-start.1 = (f32[48,8192]{1,0:T(8,128)S(1)}, f32[48,8192]{1,0:T(8,128)}, u32[]{:S(2)}, u32[]{:S(2)}) collective-permute-start(f32[48,8192]{1,0:T(8,128)S(1)} %add_select_fusion.8), channel_id=1, source_target_pairs={{0,2},{1,3},{2,0},{3,1},{4,6},{5,7},{6,4},{7,5},{8,10},{9,11},{10,... | collective-permute-start | bytes 4718600 | tf_op jit(solution)/shard_map/ppermute | solution.py:12
  60.6 38.2 %collective-permute-start.2 = (f32[48,8192]{1,0:T(8,128)S(1)}, f32[48,8192]{1,0:T(8,128)}, u32[]{:S(2)}, u32[]{:S(2)}) collective-permute-start(f32[48,8192]{1,0:T(8,128)S(1)} %add_select_fusion.7), channel_id=1, source_target_pairs={{0,4},{1,5},{2,6},{3,7},{4,0},{5,1},{6,2},{7,3},{8,12},{9,13},{10,... | collective-permute-start | bytes 4718600 | tf_op jit(solution)/shard_map/ppermute | solution.py:12
  100.4 1.9 copy-start.1
  100.4 70.8 %collective-permute-start.3 = (f32[48,8192]{1,0:T(8,128)S(1)}, f32[48,8192]{1,0:T(8,128)S(1)}, u32[]{:S(2)}, u32[]{:S(2)}) collective-permute-start(f32[48,8192]{1,0:T(8,128)S(1)} %add_select_fusion.6), channel_id=1, source_target_pairs={{0,8},{1,9},{2,10},{3,11},{4,12},{5,13},{6,14},{7,15},{8,0},{9,1},... | collective-permute-start | bytes 4718600 | tf_op jit(solution)/shard_map/ppermute | solution.py:12
  172.8 75.5 %collective-permute-start.4 = (f32[48,8192]{1,0:T(8,128)S(1)}, f32[48,8192]{1,0:T(8,128)}, u32[]{:S(2)}, u32[]{:S(2)}) collective-permute-start(f32[48,8192]{1,0:T(8,128)S(1)} %add_select_fusion.5), channel_id=1, source_target_pairs={{0,16},{1,17},{2,18},{3,19},{4,20},{5,21},{6,22},{7,23},{8,24},{9,... | collective-permute-start | bytes 4718600 | tf_op jit(solution)/shard_map/ppermute | solution.py:12
  249.8 36.5 %collective-permute-start.5 = (f32[48,8192]{1,0:T(8,128)S(1)}, f32[48,8192]{1,0:T(8,128)}, u32[]{:S(2)}, u32[]{:S(2)}) collective-permute-start(f32[48,8192]{1,0:T(8,128)S(1)} %add_select_fusion.4), channel_id=1, source_target_pairs={{0,32},{32,0},{64,96},{96,64},{128,160},{160,128},{192,224},{224,1... | collective-permute-start | bytes 4718600 | tf_op jit(solution)/shard_map/ppermute | solution.py:12
  287.9 1.9 copy-start.2
  287.9 35.5 %collective-permute-start.6 = (f32[48,8192]{1,0:T(8,128)S(1)}, f32[48,8192]{1,0:T(8,128)S(1)}, u32[]{:S(2)}, u32[]{:S(2)}) collective-permute-start(f32[48,8192]{1,0:T(8,128)S(1)} %add_select_fusion.3), channel_id=1, source_target_pairs={{0,64},{32,96},{64,0},{96,32},{128,192},{160,224},{192,128},{224,1... | collective-permute-start | bytes 4718600 | tf_op jit(solution)/shard_map/ppermute | solution.py:12
  324.9 72.9 %collective-permute-start.7 = (f32[48,8192]{1,0:T(8,128)S(1)}, f32[48,8192]{1,0:T(8,128)}, u32[]{:S(2)}, u32[]{:S(2)}) collective-permute-start(f32[48,8192]{1,0:T(8,128)S(1)} %add_select_fusion.2), channel_id=1, source_target_pairs={{0,128},{32,160},{64,192},{96,224},{128,0},{160,32},{192,64},{224,... | collective-permute-start | bytes 4718600 | tf_op jit(solution)/shard_map/ppermute | solution.py:12
  326.9 76.7 %copy-start.3 = (s32[12288]{0:T(1024)S(1)}, s32[12288]{0:T(1024)}, u32[]{:S(2)}) copy-start(s32[12288]{0:T(1024)} %param.5) | copy-start | bytes 147460
  399.4 89.4 %collective-permute-start.8 = (f32[48,8192]{1,0:T(8,128)S(1)}, f32[48,8192]{1,0:T(8,128)S(1)}, u32[]{:S(2)}, u32[]{:S(2)}) collective-permute-start(f32[48,8192]{1,0:T(8,128)S(1)} %add_select_fusion.1), channel_id=1, source_target_pairs={{0,256},{32,288},{64,320},{96,352},{128,384},{160,416},{192,448},{... | collective-permute-start | bytes 4718600 | tf_op jit(solution)/shard_map/ppermute | solution.py:12
  489.1 1.1 copy-start
  591.9 6.4 %copy-start.4 = (f32[48,48]{1,0:T(8,128)}, f32[48,48]{1,0:T(8,128)S(1)}, u32[]{:S(2)}) copy-start(f32[48,48]{1,0:T(8,128)S(1)} %copy.8) | copy-start | bytes 27652
where the time goes:
time: 599 us; the launch traced here: 598 us
  waiting for transfers between devices  352 us (59%)
  other arithmetic  107 us (18%)
  blocking collectives  99.9 us (17%)
  starting transfers between devices  30.7 us (5%)
    ppermute x9, waiting for transfers between devices, from_partner(): lax.ppermute(x, axis, [(i, i ^ 1 << apart) for i in range(lax.axis_size(a...  352 us
    psum x1, blocking collectives, per_device(): gram = lax.psum(partial_gram, ('group', 'dev')) / jnp.float32(SAMPLES)  99.9 us
    scatter-add x1, other arithmetic, per_device(): hits = jnp.zeros((rows,), jnp.float32).at[jnp.clip(local_index, 0, rows -...  85.2 us
    ppermute x9, starting transfers between devices, from_partner(): lax.ppermute(x, axis, [(i, i ^ 1 << apart) for i in range(lax.axis_size(a...  30.7 us
    select_n x8, other arithmetic, per_device(): field = jnp.where(upper, partner - field, field + partner)  13.4 us
  transfers between devices with their start and end apart: 9, of which 8 were waited for; matrix products, arithmetic and copies ran while one was open for 14% of the time, Pallas kernels for 0%

commit v1 on v0

v1 whole, which is shorter than its diff:
```python
import math

import jax
import jax.numpy as jnp
import numpy as np
from jax import lax
from jax.experimental import pallas as pl
from jax.experimental.pallas import tpu as pltpu
from jax.sharding import PartitionSpec as P

SAMPLES = 12288
AXES = ("group", "dev")
LANES = 128
A_LO = 16
VMEM = pl.BlockSpec(memory_space=pltpu.VMEM)
SMEM = pl.BlockSpec(memory_space=pltpu.SMEM)


def walsh(length):
    index = np.arange(length)
    anded = index[:, None] & index[None, :]
    parity = np.zeros((length, length), np.int32)
    for bit in range(length.bit_length() - 1):
        parity ^= anded >> bit & 1
    return (1 - 2 * parity).astype(jnp.bfloat16)


def split3(x):
    hi = x.astype(jnp.bfloat16)
    rest = x - hi.astype(jnp.float32)
    mid = rest.astype(jnp.bfloat16)
    lo = (rest - mid.astype(jnp.float32)).astype(jnp.bfloat16)
    return hi, mid, lo


def dot_nt(x, y):
    return lax.dot_general(x, y, (((1,), (1,)), ((), ())), preferred_element_type=jnp.float32)


def dot_nn(x, y):
    return lax.dot_general(x, y, (((1,), (0,)), ((), ())), preferred_element_type=jnp.float32)


def local_kernel(scale, slab_ref, flips_ref, table_ref, out_ref, field_ref):
    width, rows = slab_ref.shape
    outer = rows // LANES
    signs = (1 - 2 * flips_ref[...]).astype(jnp.float32) * scale
    for tile in range(0, width, 8):
        rows8 = pl.ds(tile, 8)
        for first in range(outer // 8):
            parts = []
            for k in range(8):
                a = k * (outer // 8) + first
                parts.append(slab_ref[rows8, pl.ds(a * LANES, LANES)] * signs[a : a + 1, :])
            for half in (4, 2, 1):
                parts = butterfly(parts, half)
            for k in range(8):
                a = k * (outer // 8) + first
                field_ref[rows8, pl.ds(a * LANES, LANES)] = parts[k]
        for first in range(0, outer, 8):
            parts = [field_ref[rows8, pl.ds((first + k) * LANES, LANES)] for k in range(8)]
            for half in (4, 2, 1):
                parts = butterfly(parts, half)
            for k in range(8):
                field_ref[rows8, pl.ds((first + k) * LANES, LANES)] = parts[k]
    table = table_ref[...]
    per = width * A_LO // LANES
    for a_hi in range(outer // A_LO):
        block = jnp.concatenate(
            [field_ref[:, pl.ds((a_hi * A_LO + a) * LANES, LANES)] for a in range(A_LO)], axis=0
        )
        hi, mid, lo = split3(block)
        turned = dot_nt(table, jnp.concatenate([hi, mid], axis=1)) + dot_nt(table[:, :LANES], lo)
        for j in range(per):
            out_ref[pl.ds(a_hi * LANES * per + j, LANES, stride=per), :] = turned[:, j * LANES : (j + 1) * LANES]


def butterfly(parts, half):
    out = list(parts)
    for k in range(len(parts)):
        if not k & half:
            out[k] = parts[k] + parts[k | half]
            out[k | half] = parts[k] - parts[k | half]
    return out


def blocks_kernel(x_ref, table_ref, out_ref):
    blocks = table_ref.shape[0]
    per = x_ref.shape[0] // blocks
    table = table_ref[...]
    for j in range(0, per, 2):
        x = jnp.concatenate([x_ref[pl.ds(j + i, blocks, stride=per), :] for i in range(2)], axis=1)
        hi, mid, lo = split3(x)
        y = dot_nn(table, hi) + dot_nn(table, mid) + dot_nn(table, lo)
        for i in range(2):
            out_ref[pl.ds(j + i, blocks, stride=per), :] = y[:, i * LANES : (i + 1) * LANES]


def hits_kernel(local_bits, me_ref, sampled_ref, out_ref):
    me = me_ref[0]
    s = sampled_ref[...]
    low = s & ((1 << local_bits) - 1)
    block = s >> local_bits
    a = low >> 7
    owner = (a // A_LO) * LANES + (low & (LANES - 1))
    row = jnp.where(owner == me, (a & (A_LO - 1)) * 4 + (block >> 7), -1)
    col = block & (LANES - 1)
    total = jnp.zeros(out_ref.shape, jnp.float32)
    rows_iota = lax.broadcasted_iota(jnp.int32, out_ref.shape, 0)
    cols_iota = lax.broadcasted_iota(jnp.int32, (LANES, LANES), 0)
    for start in range(0, s.shape[0], 8):
        ones_r, ones_c = [], []
        for k in range(start, start + 8):
            ones_r.append(jnp.where(rows_iota == row[k : k + 1, :], 1.0, 0.0).astype(jnp.bfloat16))
            ones_c.append(jnp.where(cols_iota == col[k : k + 1, :], 1.0, 0.0).astype(jnp.bfloat16))
        total = total + dot_nt(jnp.concatenate(ones_r, axis=1), jnp.concatenate(ones_c, axis=1))
    out_ref[...] = total


def gram_kernel(width, blocks, y_ref, hits_ref, out_ref, turned_ref):
    per = y_ref.shape[0] // blocks
    for j in range(per):
        turned_ref[pl.ds(j * LANES, LANES), :] = y_ref[pl.ds(j, blocks, stride=per), :].T
    total = jnp.zeros((3 * width, 3 * width), jnp.float32)
    for a_lo in range(A_LO):
        stacked = []
        for k in range(blocks // LANES):
            picked = (
                turned_ref[pl.ds(a_lo * width, width), pl.ds(k * LANES, LANES)]
                * hits_ref[pl.ds(a_lo * 4 + k, 1), :]
            )
            stacked.append(jnp.concatenate(split3(picked), axis=0))
        stacked = jnp.concatenate(stacked, axis=1)
        total = total + dot_nt(stacked, stacked)
    gram = jnp.zeros((width, width), jnp.float32)
    for i, k in ((2, 0), (0, 2), (1, 1), (1, 0), (0, 1), (0, 0)):
        gram = gram + total[i * width : (i + 1) * width, k * width : (k + 1) * width]
    out_ref[...] = gram


def turn_kernel(width, z_ref, out_ref):
    per = width * A_LO // LANES
    for a_hi in range(z_ref.shape[0] // (LANES * per)):
        turned = jnp.concatenate(
            [z_ref[pl.ds(a_hi * LANES * per + j, LANES, stride=per), :].T for j in range(per)], axis=0
        )
        for a_lo in range(A_LO):
            out_ref[:, pl.ds((a_hi * A_LO + a_lo) * LANES, LANES)] = turned[a_lo * width : (a_lo + 1) * width, :]


def call(kernel, shape, *operands, specs=None, scratch=(), name=None):
    return pl.pallas_call(
        kernel,
        out_shape=jax.ShapeDtypeStruct(shape, jnp.float32),
        in_specs=specs or [VMEM] * len(operands),
        out_specs=VMEM,
        scratch_shapes=list(scratch),
        compiler_params=pltpu.CompilerParams(vmem_limit_bytes=48 * 1024 * 1024),
        name=name,
    )(*operands)


def exchange(x, blocks):
    shape = x.shape
    x = lax.all_to_all(x.reshape(blocks, x.size // blocks), AXES, 0, 0, tiled=True)
    return x.reshape(shape)


def everywhere(x, axis):
    count = lax.axis_size(axis)
    x = jnp.broadcast_to(x[None], (count,) + x.shape)
    return jnp.sum(lax.all_to_all(x, axis, 0, 0, tiled=True), axis=0)


def per_device(slab, flips, sampled):
    width, rows = slab.shape
    blocks = lax.axis_size("group") * lax.axis_size("dev")
    scale = 1.0 / math.sqrt(rows * blocks)
    me = lax.axis_index(AXES).astype(jnp.int32).reshape(1)
    lines = width * rows // LANES

    table = walsh(LANES)
    local = call(
        lambda *refs: local_kernel(scale, *refs),
        (lines, LANES),
        slab,
        flips.reshape(rows // LANES, LANES),
        jnp.asarray(np.concatenate([table, table], axis=1)),
        scratch=[pltpu.VMEM((width, rows), jnp.float32)],
        name="local_transform",
    )
    there = exchange(local, blocks)
    hits = call(
        lambda *refs: hits_kernel(rows.bit_length() - 1, *refs),
        (A_LO * blocks // LANES, LANES),
        me,
        sampled.reshape(SAMPLES // LANES, LANES),
        specs=[SMEM, VMEM],
        name="sampled_hits",
    )
    whole = call(blocks_kernel, (lines, LANES), there, jnp.asarray(walsh(blocks)), name="block_transform")
    back = exchange(whole, blocks)
    mixed = call(lambda *refs: turn_kernel(width, *refs), (width, rows), back, name="turn_back")

    partial = call(
        lambda *refs: gram_kernel(width, blocks, *refs),
        (width, width),
        whole,
        hits,
        scratch=[pltpu.VMEM((width * A_LO, blocks), jnp.float32)],
        name="gram_terms",
    )
    total = everywhere(everywhere(partial, "group"), "dev")
    gram = total / jnp.float32(SAMPLES)
    factor = jnp.linalg.cholesky(gram).T
    return (mixed, gram, factor)


def solution(mesh):
    placed = (P(None, AXES), P(AXES), P())
    return jax.shard_map(
        per_device,
        mesh=mesh,
        in_specs=placed,
        out_specs=(P(None, AXES), P(), P()),
        check_vma=False,
    )
```

time: 599 us -> 167 us (0.28)
  waiting for transfers between devices: 352 us -> 77.5 us
  other arithmetic: 107 us -> 8.16 us
  blocking collectives: 99.9 us -> 32.2 us
  Pallas kernels: 0 us -> 10.4 us
    ppermute x9 -> x0, waiting for transfers between devices: 352 us -> none  [from_partner(): lax.ppermute(x, axis, [(i, i ^ 1 << apart) for i in range(lax.axis_size(a...]
    psum x1 -> x0, blocking collectives: 99.9 us -> none  [per_device(): gram = lax.psum(partial_gram, ('group', 'dev')) / jnp.float32(SAMPLES)]
    scatter-add x1 -> x0, other arithmetic: 85.2 us -> none  [per_device(): hits = jnp.zeros((rows,), jnp.float32).at[jnp.clip(local_index, 0, rows -...]
    all_to_all x0 -> x2, waiting for transfers between devices: none -> 77.5 us  [exchange(): lax.all_to_all(x.reshape(blocks, x.size // blocks), AXES, 0, 0, tiled=True)]
    all_to_all x0 -> x2, blocking collectives: none -> 32.2 us  [everywhere(): return jnp.sum(lax.all_to_all(x, axis, 0, 0, tiled=True), axis=0)]
    ppermute x9 -> x0, starting transfers between devices: 30.7 us -> none  [from_partner(): lax.ppermute(x, axis, [(i, i ^ 1 << apart) for i in range(lax.axis_size(a...]
    all_to_all x0 -> x2, starting transfers between devices: none -> 30.7 us  [exchange(): lax.all_to_all(x.reshape(blocks, x.size // blocks), AXES, 0, 0, tiled=True)]
    select_n x9 -> x0, other arithmetic: 13.4 us -> none  [the longest x8 13.4 us: per_device(): field = jnp.where(upper, partner - field, field + partner)]
  transfers between devices with their start and end apart: 9 -> 2, of which waited for: 8 -> 2; matrix products, arithmetic and copies ran while one was open for 14% -> 5% of each run, Pallas kernels for 0% -> 1%
where the time goes in v1:
time: 167 us; the launch traced here: 166 us
  waiting for transfers between devices  77.5 us (46%)
  blocking collectives  32.2 us (19%)
  starting transfers between devices  30.7 us (18%)
  Pallas kernels  10.4 us (6%)
  other arithmetic  8.16 us (5%)
  local copies, waits for them, and re-layouts  6.24 us (4%)
    all_to_all x2, waiting for transfers between devices, exchange(): lax.all_to_all(x.reshape(blocks, x.size // blocks), AXES, 0, 0, tiled=True)  77.5 us
    all_to_all x2, blocking collectives, everywhere(): return jnp.sum(lax.all_to_all(x, axis, 0, 0, tiled=True), axis=0)  32.2 us
    all_to_all x2, starting transfers between devices, exchange(): lax.all_to_all(x.reshape(blocks, x.size // blocks), AXES, 0, 0, tiled=True)  30.7 us
    pallas_call x5, Pallas kernels, call(): pl.pallas_call(kernel, out_shape=jax.ShapeDtypeStruct(shape, jnp.float32)...  10.4 us
    unnamed x18, local copies, waits for them, and re-layouts  5.58 us
    another operation x3, other arithmetic, per_device(): factor = jnp.linalg.cholesky(gram).T  5.05 us
  transfers between devices with their start and end apart: 2, of which 2 were waited for; matrix products, arithmetic and copies ran while one was open for 5% of the time, Pallas kernels for 1%

profile of v1, /device:TPU:1, one launch (start us, length us, event | category | flops | bytes accessed | tf_op | source)
XLA Modules:
  0.0 166.1 jit_solution(1743784882041504340)
XLA Ops:
  0.6 0.0 copy-start
  0.6 1.4 copy-done
  2.0 0.8 copy-done.2
  2.9 0.8 copy-done.4
  3.6 2.6 %local_transform.1 = f32[3072,128]{1,0:T(8,128)} custom-call(f32[48,8192]{1,0:T(8,128)S(1)} %copy-done, s32[64,128]{1,0:T(8,128)S(1)} %bitcast.16, bf16[128,256]{1,0:T(8,128)(2,1)S(1)} %copy-done.2), custom_call_target="tpu_custom_call" | custom-call | tf_op jit(solution)/shard_map/local_transform/pallas_call | solution.py:152
  6.3 22.2 %all-to-all-start = ((f32[512,1,768]{2,1,0:T(1,128)}), f32[512,1,768]{2,1,0:T(1,128)S(1)}, u32[]{:S(2)}, u32[]{:S(2)}) async-start(f32[512,1,768]{2,1,0:T(1,128)} %bitcast.1), calls=%async_computation | async-start | bytes 3145728 | tf_op jit(solution)/shard_map/all_to_all | solution.py:165
  28.5 0.0 copy-done.3
  28.5 1.2 sampled_hits.1.refs_1_
  29.7 42.6 %all-to-all-done = f32[512,1,768]{2,1,0:T(1,128)S(1)} async-done(((f32[512,1,768]{2,1,0:T(1,128)}), f32[512,1,768]{2,1,0:T(1,128)S(1)}, u32[]{:S(2)}, u32[]{:S(2)}) %all-to-all-start) | async-done | bytes 1572896 | tf_op jit(solution)/shard_map/all_to_all | solution.py:165
  72.3 0.0 copy-done.1
  72.3 2.6 %block_transform.1.refs_0_ = f32[3072,128]{1,0:T(8,128)} custom-call(f32[3072,128]{1,0:T(8,128)S(1)} %bitcast.14, bf16[512,512]{1,0:T(8,128)(2,1)S(1)} %copy-done.1), custom_call_target="tpu_custom_call" | custom-call | tf_op jit(solution)/shard_map/block_transform/pallas_call | solution.py:152
  74.9 2.4 %gram_terms.1 = f32[48,48]{1,0:T(8,128)S(1)} custom-call(f32[3072,128]{1,0:T(8,128)} %block_transform.1.refs_0_, f32[64,128]{1,0:T(8,128)S(1)} %sampled_hits.1.refs_1_), custom_call_target="tpu_custom_call" | custom-call | tf_op jit(solution)/shard_map/gram_terms/pallas_call | solution.py:152
  77.3 0.4 reshape.44
  77.7 11.8 %all_to_all.28 = f32[16,1,2304]{2,1,0:T(1,128)S(1)} all-to-all(f32[16,1,2304]{2,1,0:T(1,128)S(1)} %reshape.44), channel_id=1, replica_groups=mesh['group'=16,'dev'=32] {'group'}, dimensions={0} | all-to-all | bytes 294912 | tf_op jit(solution)/shard_map/all_to_all | solution.py:172
  89.5 0.5 broadcast.41
  90.0 1.0 reduce.6
  91.0 0.2 reshape.45
  91.3 0.1 broadcast_in_dim.6
  91.4 0.7 reshape.46
  92.1 20.4 %all_to_all.29 = f32[32,1,2304]{2,1,0:T(1,128)S(1)} all-to-all(f32[32,1,2304]{2,1,0:T(1,128)S(1)} %reshape.46), channel_id=1, replica_groups=mesh['group'=16,'dev'=32] {'dev'}, dimensions={0} | all-to-all | bytes 589824 | tf_op jit(solution)/shard_map/all_to_all | solution.py:172
  112.5 8.6 %all-to-all-start.1 = ((f32[512,1,768]{2,1,0:T(1,128)}), f32[512,1,768]{2,1,0:T(1,128)S(1)}, u32[]{:S(2)}, u32[]{:S(2)}) async-start(f32[512,1,768]{2,1,0:T(1,128)} %bitcast.3), calls=%async_computation.1 | async-start | bytes 3145728 | tf_op jit(solution)/shard_map/all_to_all | solution.py:165
  121.1 1.3 reduce.7
  122.4 0.5 reshape.47
  122.9 0.1 reduce_sum.19
  123.0 0.1 copy.18
  123.1 0.1 copy.20
  123.2 4.4 %cholesky.18 = f32[48,48]{1,0:T(8,128)S(1)} custom-call(f32[48,48]{1,0:T(8,128)S(1)} %fusion), custom_call_target="Cholesky" | custom-call | tf_op jit(solution)/shard_map/jit(cholesky)/cholesky | solution.py:215
  127.6 0.6 compare_reduce_fusion
  128.3 0.7 select_bitcast_fusion
  128.9 0.7 copy.21
  129.6 34.9 %all-to-all-done.1 = f32[512,1,768]{2,1,0:T(1,128)S(1)} async-done(((f32[512,1,768]{2,1,0:T(1,128)}), f32[512,1,768]{2,1,0:T(1,128)S(1)}, u32[]{:S(2)}, u32[]{:S(2)}) %all-to-all-start.1) | async-done | bytes 1572896 | tf_op jit(solution)/shard_map/all_to_all | solution.py:165
  164.5 1.6 turn_back.1
  (11 shorter events, 0.1 us)
Async XLA Ops:
  0.6 1.4 copy-start
  2.0 0.8 copy-start.2
  2.9 0.8 copy-start.4
  6.3 22.2 %copy-start.3 = (s32[12288]{0:T(1024)S(1)}, s32[12288]{0:T(1024)}, u32[]{:S(2)}) copy-start(s32[12288]{0:T(1024)} %param.7) | copy-start | bytes 147460
  6.3 66.1 %copy-start.1 = (bf16[512,512]{1,0:T(8,128)(2,1)S(1)}, bf16[512,512]{1,0:T(8,128)(2,1)}, u32[]{:S(2)}) copy-start(bf16[512,512]{1,0:T(8,128)(2,1)} %constant.57.clone.table_ref) | copy-start | bytes 1572868
  6.3 66.1 %all-to-all-start = ((f32[512,1,768]{2,1,0:T(1,128)}), f32[512,1,768]{2,1,0:T(1,128)S(1)}, u32[]{:S(2)}, u32[]{:S(2)}) async-start(f32[512,1,768]{2,1,0:T(1,128)} %bitcast.1), calls=%async_computation | async-start | bytes 3145728 | tf_op jit(solution)/shard_map/all_to_all | solution.py:165
  112.5 52.0 %all-to-all-start.1 = ((f32[512,1,768]{2,1,0:T(1,128)}), f32[512,1,768]{2,1,0:T(1,128)S(1)}, u32[]{:S(2)}, u32[]{:S(2)}) async-start(f32[512,1,768]{2,1,0:T(1,128)} %bitcast.3), calls=%async_computation.1 | async-start | bytes 3145728 | tf_op jit(solution)/shard_map/all_to_all | solution.py:165
  123.2 42.9 %copy-start.5 = (f32[48,48]{1,0:T(8,128)}, f32[48,48]{1,0:T(8,128)S(1)}, u32[]{:S(2)}) copy-start(f32[48,48]{1,0:T(8,128)S(1)} %copy.20) | copy-start | bytes 27652

commit v2 on v1

--- a/solution.py
+++ b/solution.py
@@ -12,7 +12,10 @@
 AXES = ("group", "dev")
 LANES = 128
 A_LO = 16
+PACK = 16
+PIVOTS = 4
 VMEM = pl.BlockSpec(memory_space=pltpu.VMEM)
+HBM = pl.BlockSpec(memory_space=pltpu.HBM)
 SMEM = pl.BlockSpec(memory_space=pltpu.SMEM)
 
 
@@ -41,17 +44,35 @@
     return lax.dot_general(x, y, (((1,), (0,)), ((), ())), preferred_element_type=jnp.float32)
 
 
-def local_kernel(scale, slab_ref, flips_ref, table_ref, out_ref, field_ref):
+def walsh_in_kernel(shape):
+    anded = lax.broadcasted_iota(jnp.int32, shape, 0) & lax.broadcasted_iota(jnp.int32, shape, 1)
+    for shift in (4, 2, 1):
+        anded = anded ^ anded >> shift
+    return (1 - 2 * (anded & 1)).astype(jnp.float32).astype(jnp.bfloat16)
+
+
+def local_kernel(scale, slab_ref, flips_ref, out_ref, field_ref, signs_ref, turned_ref, in_sem, flip_sem, out_sem):
     width, rows = slab_ref.shape
     outer = rows // LANES
-    signs = (1 - 2 * flips_ref[...]).astype(jnp.float32) * scale
-    for tile in range(0, width, 8):
-        rows8 = pl.ds(tile, 8)
+    flips_in = pltpu.make_async_copy(flips_ref, signs_ref, flip_sem)
+    flips_in.start()
+    slab_in = []
+    for tile in range(width // 8):
+        part = pl.ds(tile * 8, 8)
+        slab_in.append(pltpu.make_async_copy(slab_ref.at[part], field_ref.at[part], in_sem.at[tile]))
+        slab_in[-1].start()
+    table = walsh_in_kernel((LANES, LANES))
+    table2 = jnp.concatenate([table, table], axis=1)
+    flips_in.wait()
+    signs = (1 - 2 * signs_ref[...]).astype(jnp.float32) * scale
+    for tile in range(width // 8):
+        rows8 = pl.ds(tile * 8, 8)
+        slab_in[tile].wait()
         for first in range(outer // 8):
             parts = []
             for k in range(8):
                 a = k * (outer // 8) + first
-                parts.append(slab_ref[rows8, pl.ds(a * LANES, LANES)] * signs[a : a + 1, :])
+                parts.append(field_ref[rows8, pl.ds(a * LANES, LANES)] * signs[a : a + 1, :])
             for half in (4, 2, 1):
                 parts = butterfly(parts, half)
             for k in range(8):
@@ -63,16 +84,21 @@
                 parts = butterfly(parts, half)
             for k in range(8):
                 field_ref[rows8, pl.ds((first + k) * LANES, LANES)] = parts[k]
-    table = table_ref[...]
     per = width * A_LO // LANES
+    out = []
     for a_hi in range(outer // A_LO):
         block = jnp.concatenate(
             [field_ref[:, pl.ds((a_hi * A_LO + a) * LANES, LANES)] for a in range(A_LO)], axis=0
         )
         hi, mid, lo = split3(block)
-        turned = dot_nt(table, jnp.concatenate([hi, mid], axis=1)) + dot_nt(table[:, :LANES], lo)
+        turned = dot_nt(table2, jnp.concatenate([hi, mid], axis=1)) + dot_nt(table, lo)
         for j in range(per):
-            out_ref[pl.ds(a_hi * LANES * per + j, LANES, stride=per), :] = turned[:, j * LANES : (j + 1) * LANES]
+            turned_ref[pl.ds(a_hi * LANES * per + j, LANES, stride=per), :] = turned[:, j * LANES : (j + 1) * LANES]
+        part = pl.ds(a_hi * LANES * per, LANES * per)
+        out.append(pltpu.make_async_copy(turned_ref.at[part], out_ref.at[part], out_sem.at[a_hi]))
+        out[-1].start()
+    for copy in out:
+        copy.wait()
 
 
 def butterfly(parts, half):
@@ -84,7 +110,7 @@
     return out
 
 
-def blocks_kernel(x_ref, table_ref, out_ref):
+def blocks_kernel(width, x_ref, table_ref, hits_ref, out_ref, packed_ref, y_ref, turned_ref, out_sem):
     blocks = table_ref.shape[0]
     per = x_ref.shape[0] // blocks
     table = table_ref[...]
@@ -93,7 +119,13 @@
         hi, mid, lo = split3(x)
         y = dot_nn(table, hi) + dot_nn(table, mid) + dot_nn(table, lo)
         for i in range(2):
-            out_ref[pl.ds(j + i, blocks, stride=per), :] = y[:, i * LANES : (i + 1) * LANES]
+            part = y[:, i * LANES : (i + 1) * LANES]
+            y_ref[pl.ds(j + i, blocks, stride=per), :] = part
+            turned_ref[pl.ds((j + i) * LANES, LANES), :] = part.T
+    out = pltpu.make_async_copy(y_ref, out_ref, out_sem)
+    out.start()
+    gram_terms(width, turned_ref, hits_ref, packed_ref)
+    out.wait()
 
 
 def hits_kernel(local_bits, me_ref, sampled_ref, out_ref):
@@ -117,10 +149,8 @@
     out_ref[...] = total
 
 
-def gram_kernel(width, blocks, y_ref, hits_ref, out_ref, turned_ref):
-    per = y_ref.shape[0] // blocks
-    for j in range(per):
-        turned_ref[pl.ds(j * LANES, LANES), :] = y_ref[pl.ds(j, blocks, stride=per), :].T
+def gram_terms(width, turned_ref, hits_ref, out_ref):
+    blocks = turned_ref.shape[1]
     total = jnp.zeros((3 * width, 3 * width), jnp.float32)
     for a_lo in range(A_LO):
         stacked = []
@@ -135,25 +165,72 @@
     gram = jnp.zeros((width, width), jnp.float32)
     for i, k in ((2, 0), (0, 2), (1, 1), (1, 0), (0, 1), (0, 0)):
         gram = gram + total[i * width : (i + 1) * width, k * width : (k + 1) * width]
-    out_ref[...] = gram
-
-
-def turn_kernel(width, z_ref, out_ref):
+    out_ref[...] = jnp.zeros_like(out_ref)
+    at = 0
+    for i in range(0, width, PACK):
+        out_ref[:, pl.ds(at, width - i)] = gram[i : i + PACK, i:]
+        at += width - i
+
+
+def factor_kernel(x_ref, partner_ref, gram_ref, factor_ref, full_ref):
+    width = gram_ref.shape[0]
+    packed = (x_ref[...] + partner_ref[...]) / jnp.float32(SAMPLES)
+    full_ref[...] = jnp.zeros_like(full_ref)
+    at = 0
+    for i in range(0, width, PACK):
+        full_ref[pl.ds(i, PACK), pl.ds(i, width - i)] = packed[:, at : at + width - i]
+        at += width - i
+    for i in range(0, width, PACK):
+        for k in range(i + PACK, width, PACK):
+            full_ref[pl.ds(k, PACK), pl.ds(i, PACK)] = full_ref[pl.ds(i, PACK), pl.ds(k, PACK)].T
+    left = full_ref[...]
+    gram_ref[...] = left[:, :width]
+    lane = lax.broadcasted_iota(jnp.int32, (1, LANES), 1)
+    upper = []
+    for at in range(0, width, PIVOTS):
+        rows = [left[at + i : at + i + 1, :] for i in range(PIVOTS)]
+        cols = [jnp.broadcast_to(left[:, at + i : at + i + 1], left.shape) for i in range(PIVOTS)]
+        pivot = [
+            [jnp.broadcast_to(rows[i][:, at + k : at + k + 1], (1, LANES)) for k in range(PIVOTS)]
+            for i in range(PIVOTS)
+        ]
+        for i in range(PIVOTS):
+            inverse = 1.0 / pivot[i][i]
+            for k in range(i + 1, PIVOTS):
+                ratio = pivot[i][k] * inverse
+                rows[k] = rows[k] - ratio * rows[i]
+                cols[k] = cols[k] - ratio * cols[i]
+                for m in range(k, PIVOTS):
+                    pivot[k][m] = pivot[k][m] - ratio * pivot[i][m]
+            upper.append(jnp.where(lane >= at + i, rows[i] / jnp.sqrt(pivot[i][i]), 0.0))
+            left = left - cols[i] * (rows[i] * inverse)
+    for i in range(width):
+        factor_ref[pl.ds(i, 1), :] = upper[i][:, :width]
+
+
+def turn_kernel(width, z_ref, out_ref, turned_ref, out_sem):
     per = width * A_LO // LANES
+    out = []
     for a_hi in range(z_ref.shape[0] // (LANES * per)):
         turned = jnp.concatenate(
             [z_ref[pl.ds(a_hi * LANES * per + j, LANES, stride=per), :].T for j in range(per)], axis=0
         )
         for a_lo in range(A_LO):
-            out_ref[:, pl.ds((a_hi * A_LO + a_lo) * LANES, LANES)] = turned[a_lo * width : (a_lo + 1) * width, :]
-
-
-def call(kernel, shape, *operands, specs=None, scratch=(), name=None):
+            turned_ref[:, pl.ds((a_hi * A_LO + a_lo) * LANES, LANES)] = turned[a_lo * width : (a_lo + 1) * width, :]
+        part = (slice(None), pl.ds(a_hi * A_LO * LANES, A_LO * LANES))
+        out.append(pltpu.make_async_copy(turned_ref.at[part], out_ref.at[part], out_sem.at[a_hi]))
+        out[-1].start()
+    for copy in out:
+        copy.wait()
+
+
+def call(kernel, shapes, *operands, specs=None, out_specs=None, scratch=(), name=None):
+    out = [jax.ShapeDtypeStruct(shape, jnp.float32) for shape in shapes]
     return pl.pallas_call(
         kernel,
-        out_shape=jax.ShapeDtypeStruct(shape, jnp.float32),
+        out_shape=out,
         in_specs=specs or [VMEM] * len(operands),
-        out_specs=VMEM,
+        out_specs=out_specs or [VMEM] * len(out),
         scratch_shapes=list(scratch),
         compiler_params=pltpu.CompilerParams(vmem_limit_bytes=48 * 1024 * 1024),
         name=name,
@@ -166,10 +243,19 @@
     return x.reshape(shape)
 
 
-def everywhere(x, axis):
+def sum_over(x, axis):
     count = lax.axis_size(axis)
     x = jnp.broadcast_to(x[None], (count,) + x.shape)
     return jnp.sum(lax.all_to_all(x, axis, 0, 0, tiled=True), axis=0)
+
+
+def sum_pairwise(x, axis):
+    count = lax.axis_size(axis)
+    partner = jnp.zeros_like(x)
+    for bit in range(count.bit_length() - 1):
+        x = x + partner if bit else x
+        partner = lax.ppermute(x, axis, [(i, i ^ 1 << bit) for i in range(count)])
+    return x, partner
 
 
 def per_device(slab, flips, sampled):
@@ -178,41 +264,62 @@
     scale = 1.0 / math.sqrt(rows * blocks)
     me = lax.axis_index(AXES).astype(jnp.int32).reshape(1)
     lines = width * rows // LANES
-
-    table = walsh(LANES)
-    local = call(
+    outer = rows // LANES
+    dma = pltpu.SemaphoreType.DMA
+
+    (local,) = call(
         lambda *refs: local_kernel(scale, *refs),
-        (lines, LANES),
+        [(lines, LANES)],
         slab,
-        flips.reshape(rows // LANES, LANES),
-        jnp.asarray(np.concatenate([table, table], axis=1)),
-        scratch=[pltpu.VMEM((width, rows), jnp.float32)],
+        flips.reshape(outer, LANES),
+        specs=[HBM, HBM],
+        out_specs=[HBM],
+        scratch=[
+            pltpu.VMEM((width, rows), jnp.float32),
+            pltpu.VMEM((outer, LANES), jnp.int32),
+            pltpu.VMEM((lines, LANES), jnp.float32),
+            dma((width // 8,)),
+            dma,
+            dma((outer // A_LO,)),
+        ],
         name="local_transform",
     )
     there = exchange(local, blocks)
-    hits = call(
+    (hits,) = call(
         lambda *refs: hits_kernel(rows.bit_length() - 1, *refs),
-        (A_LO * blocks // LANES, LANES),
+        [(A_LO * blocks // LANES, LANES)],
         me,
         sampled.reshape(SAMPLES // LANES, LANES),
         specs=[SMEM, VMEM],
         name="sampled_hits",
     )
-    whole = call(blocks_kernel, (lines, LANES), there, jnp.asarray(walsh(blocks)), name="block_transform")
+    whole, partial = call(
+        lambda *refs: blocks_kernel(width, *refs),
+        [(lines, LANES), (PACK, LANES)],
+        there,
+        jnp.asarray(walsh(blocks)),
+        hits,
+        out_specs=[HBM, VMEM],
+        scratch=[pltpu.VMEM((lines, LANES), jnp.float32), pltpu.VMEM((width * A_LO, blocks), jnp.float32), dma],
+        name="block_transform",
+    )
+    whole, partial = lax.optimization_barrier((whole, sum_over(partial, "group")))
     back = exchange(whole, blocks)
-    mixed = call(lambda *refs: turn_kernel(width, *refs), (width, rows), back, name="turn_back")
-
-    partial = call(
-        lambda *refs: gram_kernel(width, blocks, *refs),
-        (width, width),
-        whole,
-        hits,
-        scratch=[pltpu.VMEM((width * A_LO, blocks), jnp.float32)],
-        name="gram_terms",
-    )
-    total = everywhere(everywhere(partial, "group"), "dev")
-    gram = total / jnp.float32(SAMPLES)
-    factor = jnp.linalg.cholesky(gram).T
+    (mixed,) = call(
+        lambda *refs: turn_kernel(width, *refs),
+        [(width, rows)],
+        back,
+        out_specs=[HBM],
+        scratch=[pltpu.VMEM((width, rows), jnp.float32), dma((outer // A_LO,))],
+        name="turn_back",
+    )
+    gram, factor = call(
+        factor_kernel,
+        [(width, width)] * 2,
+        *sum_pairwise(partial, "dev"),
+        scratch=[pltpu.VMEM((width, LANES), jnp.float32)],
+        name="factor",
+    )
     return (mixed, gram, factor)
 
 

time: 167 us -> 143 us (0.86)
  blocking collectives: 32.2 us -> 11.7 us
  starting transfers between devices: 30.7 us -> 47.7 us
  other arithmetic: 8.16 us -> 0.03 us
  waiting for transfers between devices: 77.5 us -> 69.4 us
  local copies, waits for them, and re-layouts: 6.24 us -> 2.18 us
    all_to_all x2, waiting for transfers between devices: 77.5 us -> 48.8 us  [exchange(): lax.all_to_all(x.reshape(blocks, x.size // blocks), AXES, 0, 0, tiled=True)]
    ppermute x0 -> x5, waiting for transfers between devices: none -> 20.7 us  [sum_pairwise(): partner = lax.ppermute(x, axis, [(i, i ^ 1 << bit) for i in range(count)])]
    all_to_all x2 -> x1, blocking collectives: 32.2 us -> 11.7 us  [sum_over(): return jnp.sum(lax.all_to_all(x, axis, 0, 0, tiled=True), axis=0)]
    ppermute x0 -> x5, starting transfers between devices: none -> 15 us  [sum_pairwise(): partner = lax.ppermute(x, axis, [(i, i ^ 1 << bit) for i in range(count)])]
    another operation x3 -> x0, other arithmetic: 5.05 us -> none  [per_device(): factor = jnp.linalg.cholesky(gram).T]
    unnamed x18 -> x8, local copies, waits for them, and re-layouts: 5.58 us -> 2.17 us
    all_to_all x2 -> x0, other arithmetic: 2.33 us -> none  [everywhere(): return jnp.sum(lax.all_to_all(x, axis, 0, 0, tiled=True), axis=0)]
    all_to_all x2, starting transfers between devices: 30.7 us -> 32.7 us  [exchange(): lax.all_to_all(x.reshape(blocks, x.size // blocks), AXES, 0, 0, tiled=True)]
  transfers between devices with their start and end apart: 2 -> 7, of which waited for: 2 -> 7; matrix products, arithmetic and copies ran while one was open for 5% -> 0% of each run, Pallas kernels for 1% -> 2%
where the time goes in v2:
time: 143 us; the launch traced here: 142 us
  waiting for transfers between devices  69.4 us (49%)
  starting transfers between devices  47.7 us (33%)
  blocking collectives  11.7 us (8%)
  Pallas kernels  10.4 us (7%)
  local copies, waits for them, and re-layouts  2.18 us (2%)
    all_to_all x2, waiting for transfers between devices, exchange(): lax.all_to_all(x.reshape(blocks, x.size // blocks), AXES, 0, 0, tiled=True)  48.8 us
    all_to_all x2, starting transfers between devices, exchange(): lax.all_to_all(x.reshape(blocks, x.size // blocks), AXES, 0, 0, tiled=True)  32.7 us
    ppermute x5, waiting for transfers between devices, sum_pairwise(): partner = lax.ppermute(x, axis, [(i, i ^ 1 << bit) for i in range(count)])  20.7 us
    ppermute x5, starting transfers between devices, sum_pairwise(): partner = lax.ppermute(x, axis, [(i, i ^ 1 << bit) for i in range(count)])  15 us
    all_to_all x1, blocking collectives, sum_over(): return jnp.sum(lax.all_to_all(x, axis, 0, 0, tiled=True), axis=0)  11.7 us
    pallas_call x5, Pallas kernels, call(): pl.pallas_call(kernel, out_shape=out, in_specs=specs or [VMEM] * len(oper...  10.4 us
  transfers between devices with their start and end apart: 7, of which 7 were waited for; matrix products, arithmetic and copies ran while one was open for 0% of the time, Pallas kernels for 2%

profile of v2, /device:TPU:1, one launch (start us, length us, event | category | flops | bytes accessed | tf_op | source)
XLA Modules:
  0.0 142.2 jit_solution(5722492994326428993)
XLA Ops:
  0.6 0.0 copy-start
  0.6 1.4 copy-done
  2.0 0.0 copy-start.3
  2.0 0.8 copy-done.3
  2.8 2.5 %local_transform.1 = f32[3072,128]{1,0:T(8,128)} custom-call(f32[48,8192]{1,0:T(8,128)S(1)} %copy-done, s32[64,128]{1,0:T(8,128)S(1)} %bitcast.10), custom_call_target="tpu_custom_call" | custom-call | tf_op jit(solution)/shard_map/local_transform/pallas_call | solution.py:229
  5.3 0.0 copy-start.2
  5.3 0.0 copy-start.1
  5.3 22.2 %all-to-all-start = ((f32[512,1,768]{2,1,0:T(1,128)}), f32[512,1,768]{2,1,0:T(1,128)S(1)}, u32[]{:S(2)}, u32[]{:S(2)}) async-start(f32[512,1,768]{2,1,0:T(1,128)} %bitcast.1), calls=%async_computation | async-start | bytes 3145728 | tf_op jit(solution)/shard_map/all_to_all | solution.py:242
  27.5 0.0 copy-done.2
  27.5 1.2 sampled_hits.1.refs_2_
  28.8 42.6 %all-to-all-done = f32[512,1,768]{2,1,0:T(1,128)S(1)} async-done(((f32[512,1,768]{2,1,0:T(1,128)}), f32[512,1,768]{2,1,0:T(1,128)S(1)}, u32[]{:S(2)}, u32[]{:S(2)}) %all-to-all-start) | async-done | bytes 1572896 | tf_op jit(solution)/shard_map/all_to_all | solution.py:242
  71.4 0.0 copy-done.1
  71.4 3.2 %block_transform.1 = (f32[3072,128]{1,0:T(8,128)}, f32[16,128]{1,0:T(8,128)S(1)}) custom-call(f32[3072,128]{1,0:T(8,128)S(1)} %bitcast.8, bf16[512,512]{1,0:T(8,128)(2,1)S(1)} %copy-done.1, f32[64,128]{1,0:T(8,128)S(1)} %sampled_hits.1.refs_2_), custom_call_target="tpu_custom_call" | custom-call | tf_op jit(solution)/shard_map/block_transform/pallas_call | solution.py:229
  74.6 11.7 %all_to_all.23 = f32[16,16,128]{2,1,0:T(8,128)S(1)} all-to-all(f32[16,16,128]{2,1,0:T(8,128)S(1)} %broadcast_in_dim.2), channel_id=1, replica_groups=mesh['group'=16,'dev'=32] {'group'}, dimensions={0} | all-to-all | bytes 262144 | tf_op jit(solution)/shard_map/all_to_all | solution.py:249
  86.3 10.5 %all-to-all-start.2 = ((f32[512,1,768]{2,1,0:T(1,128)}), f32[512,1,768]{2,1,0:T(1,128)S(1)}, u32[]{:S(2)}, u32[]{:S(2)}) async-start(f32[512,1,768]{2,1,0:T(1,128)} %bitcast.5), calls=%async_computation.2 | async-start | bytes 3145728 | tf_op jit(solution)/shard_map/all_to_all | solution.py:242
  96.8 6.3 %collective-permute-start = (f32[16,128]{1,0:T(8,128)S(1)}, f32[16,128]{1,0:T(8,128)S(1)}, u32[]{:S(2)}, u32[]{:S(2)}) collective-permute-start(f32[16,128]{1,0:T(8,128)S(1)} %reduce_sum.9), channel_id=1, source_target_pairs={{0,1},{1,0},{2,3},{3,2},{4,5},{5,4},{6,7},{7,6},{8,9},{9,8},{10,11... | collective-permute-start | bytes 24584 | tf_op jit(solution)/shard_map/ppermute | solution.py:257
  103.2 0.8 collective-permute-done
  104.0 1.9 %collective-permute-start.1 = (f32[16,128]{1,0:T(8,128)S(1)}, f32[16,128]{1,0:T(8,128)S(1)}, u32[]{:S(2)}, u32[]{:S(2)}) collective-permute-start(f32[16,128]{1,0:T(8,128)S(1)} %add.16), channel_id=1, source_target_pairs={{0,2},{1,3},{2,0},{3,1},{4,6},{5,7},{6,4},{7,5},{8,10},{9,11},{10,... | collective-permute-start | bytes 24584 | tf_op jit(solution)/shard_map/ppermute | solution.py:257
  105.9 3.0 %collective-permute-done.1 = f32[16,128]{1,0:T(8,128)S(1)} collective-permute-done((f32[16,128]{1,0:T(8,128)S(1)}, f32[16,128]{1,0:T(8,128)S(1)}, u32[]{:S(2)}, u32[]{:S(2)}) %collective-permute-start.1) | collective-permute-done | bytes 8224 | tf_op jit(solution)/shard_map/ppermute | solution.py:257
  108.9 1.9 %collective-permute-start.2 = (f32[16,128]{1,0:T(8,128)S(1)}, f32[16,128]{1,0:T(8,128)S(1)}, u32[]{:S(2)}, u32[]{:S(2)}) collective-permute-start(f32[16,128]{1,0:T(8,128)S(1)} %add.17), channel_id=1, source_target_pairs={{0,4},{1,5},{2,6},{3,7},{4,0},{5,1},{6,2},{7,3},{8,12},{9,13},{10,... | collective-permute-start | bytes 24584 | tf_op jit(solution)/shard_map/ppermute | solution.py:257
  110.8 4.4 %collective-permute-done.2 = f32[16,128]{1,0:T(8,128)S(1)} collective-permute-done((f32[16,128]{1,0:T(8,128)S(1)}, f32[16,128]{1,0:T(8,128)S(1)}, u32[]{:S(2)}, u32[]{:S(2)}) %collective-permute-start.2) | collective-permute-done | bytes 8224 | tf_op jit(solution)/shard_map/ppermute | solution.py:257
  115.2 1.9 %collective-permute-start.3 = (f32[16,128]{1,0:T(8,128)S(1)}, f32[16,128]{1,0:T(8,128)S(1)}, u32[]{:S(2)}, u32[]{:S(2)}) collective-permute-start(f32[16,128]{1,0:T(8,128)S(1)} %add.18), channel_id=1, source_target_pairs={{0,8},{1,9},{2,10},{3,11},{4,12},{5,13},{6,14},{7,15},{8,0},{9,1},... | collective-permute-start | bytes 24584 | tf_op jit(solution)/shard_map/ppermute | solution.py:257
  117.1 6.6 %collective-permute-done.3 = f32[16,128]{1,0:T(8,128)S(1)} collective-permute-done((f32[16,128]{1,0:T(8,128)S(1)}, f32[16,128]{1,0:T(8,128)S(1)}, u32[]{:S(2)}, u32[]{:S(2)}) %collective-permute-start.3) | collective-permute-done | bytes 8224 | tf_op jit(solution)/shard_map/ppermute | solution.py:257
  123.7 2.9 %collective-permute-start.4 = (f32[16,128]{1,0:T(8,128)S(1)}, f32[16,128]{1,0:T(8,128)S(1)}, u32[]{:S(2)}, u32[]{:S(2)}) collective-permute-start(f32[16,128]{1,0:T(8,128)S(1)} %add.19.x_ref), channel_id=1, source_target_pairs={{0,16},{1,17},{2,18},{3,19},{4,20},{5,21},{6,22},{7,23},{8,24},{9,... | collective-permute-start | bytes 24584 | tf_op jit(solution)/shard_map/ppermute | solution.py:257
  126.6 6.0 %collective-permute-done.4.partner_ref = f32[16,128]{1,0:T(8,128)S(1)} collective-permute-done((f32[16,128]{1,0:T(8,128)S(1)}, f32[16,128]{1,0:T(8,128)S(1)}, u32[]{:S(2)}, u32[]{:S(2)}) %collective-permute-start.4) | collective-permute-done | bytes 8224 | tf_op jit(solution)/shard_map/ppermute | solution.py:257
  132.5 2.2 %factor.1 = (f32[48,48]{1,0:T(8,128)}, f32[48,48]{1,0:T(8,128)}) custom-call(f32[16,128]{1,0:T(8,128)S(1)} %add.19.x_ref, f32[16,128]{1,0:T(8,128)S(1)} %collective-permute-done.4.partner_ref), custom_call_target="tpu_custom_call" | custom-call | tf_op jit(solution)/shard_map/factor/pallas_call | solution.py:229
  134.7 6.1 %all-to-all-done.2 = f32[512,1,768]{2,1,0:T(1,128)S(1)} async-done(((f32[512,1,768]{2,1,0:T(1,128)}), f32[512,1,768]{2,1,0:T(1,128)S(1)}, u32[]{:S(2)}, u32[]{:S(2)}) %all-to-all-start.2) | async-done | bytes 1572896 | tf_op jit(solution)/shard_map/all_to_all | solution.py:242
  140.8 1.3 turn_back.1
  (6 shorter events, 0.0 us)
Async XLA Ops:
  0.6 1.4 copy-start
  2.0 0.8 copy-start.3
  5.3 22.2 %copy-start.2 = (s32[12288]{0:T(1024)S(1)}, s32[12288]{0:T(1024)}, u32[]{:S(2)}) copy-start(s32[12288]{0:T(1024)} %param.6) | copy-start | bytes 147460
  5.3 66.1 %copy-start.1 = (bf16[512,512]{1,0:T(8,128)(2,1)S(1)}, bf16[512,512]{1,0:T(8,128)(2,1)}, u32[]{:S(2)}) copy-start(bf16[512,512]{1,0:T(8,128)(2,1)} %constant.15.clone.refs_1_) | copy-start | bytes 1572868
  5.3 66.1 %all-to-all-start = ((f32[512,1,768]{2,1,0:T(1,128)}), f32[512,1,768]{2,1,0:T(1,128)S(1)}, u32[]{:S(2)}, u32[]{:S(2)}) async-start(f32[512,1,768]{2,1,0:T(1,128)} %bitcast.1), calls=%async_computation | async-start | bytes 3145728 | tf_op jit(solution)/shard_map/all_to_all | solution.py:242
  86.3 54.5 %all-to-all-start.2 = ((f32[512,1,768]{2,1,0:T(1,128)}), f32[512,1,768]{2,1,0:T(1,128)S(1)}, u32[]{:S(2)}, u32[]{:S(2)}) async-start(f32[512,1,768]{2,1,0:T(1,128)} %bitcast.5), calls=%async_computation.2 | async-start | bytes 3145728 | tf_op jit(solution)/shard_map/all_to_all | solution.py:242
  96.8 7.2 %collective-permute-start = (f32[16,128]{1,0:T(8,128)S(1)}, f32[16,128]{1,0:T(8,128)S(1)}, u32[]{:S(2)}, u32[]{:S(2)}) collective-permute-start(f32[16,128]{1,0:T(8,128)S(1)} %reduce_sum.9), channel_id=1, source_target_pairs={{0,1},{1,0},{2,3},{3,2},{4,5},{5,4},{6,7},{7,6},{8,9},{9,8},{10,11... | collective-permute-start | bytes 24584 | tf_op jit(solution)/shard_map/ppermute | solution.py:257
  104.0 4.9 %collective-permute-start.1 = (f32[16,128]{1,0:T(8,128)S(1)}, f32[16,128]{1,0:T(8,128)S(1)}, u32[]{:S(2)}, u32[]{:S(2)}) collective-permute-start(f32[16,128]{1,0:T(8,128)S(1)} %add.16), channel_id=1, source_target_pairs={{0,2},{1,3},{2,0},{3,1},{4,6},{5,7},{6,4},{7,5},{8,10},{9,11},{10,... | collective-permute-start | bytes 24584 | tf_op jit(solution)/shard_map/ppermute | solution.py:257
  108.9 6.3 %collective-permute-start.2 = (f32[16,128]{1,0:T(8,128)S(1)}, f32[16,128]{1,0:T(8,128)S(1)}, u32[]{:S(2)}, u32[]{:S(2)}) collective-permute-start(f32[16,128]{1,0:T(8,128)S(1)} %add.17), channel_id=1, source_target_pairs={{0,4},{1,5},{2,6},{3,7},{4,0},{5,1},{6,2},{7,3},{8,12},{9,13},{10,... | collective-permute-start | bytes 24584 | tf_op jit(solution)/shard_map/ppermute | solution.py:257
  115.2 8.5 %collective-permute-start.3 = (f32[16,128]{1,0:T(8,128)S(1)}, f32[16,128]{1,0:T(8,128)S(1)}, u32[]{:S(2)}, u32[]{:S(2)}) collective-permute-start(f32[16,128]{1,0:T(8,128)S(1)} %add.18), channel_id=1, source_target_pairs={{0,8},{1,9},{2,10},{3,11},{4,12},{5,13},{6,14},{7,15},{8,0},{9,1},... | collective-permute-start | bytes 24584 | tf_op jit(solution)/shard_map/ppermute | solution.py:257
  123.7 8.9 %collective-permute-start.4 = (f32[16,128]{1,0:T(8,128)S(1)}, f32[16,128]{1,0:T(8,128)S(1)}, u32[]{:S(2)}, u32[]{:S(2)}) collective-permute-start(f32[16,128]{1,0:T(8,128)S(1)} %add.19.x_ref), channel_id=1, source_target_pairs={{0,16},{1,17},{2,18},{3,19},{4,20},{5,21},{6,22},{7,23},{8,24},{9,... | collective-permute-start | bytes 24584 | tf_op jit(solution)/shard_map/ppermute | solution.py:257

commit v3 on v2

--- a/solution.py
+++ b/solution.py
@@ -13,7 +13,11 @@
 LANES = 128
 A_LO = 16
 PACK = 16
-PIVOTS = 4
+FAR = (5, 6, 7, 8)
+NEAR = (0,)
+MIDDLE = (1, 2)
+LAST = (3, 4)
+PIVOTS = 8
 VMEM = pl.BlockSpec(memory_space=pltpu.VMEM)
 HBM = pl.BlockSpec(memory_space=pltpu.HBM)
 SMEM = pl.BlockSpec(memory_space=pltpu.SMEM)
@@ -110,7 +114,7 @@
     return out
 
 
-def blocks_kernel(width, x_ref, table_ref, hits_ref, out_ref, packed_ref, y_ref, turned_ref, out_sem):
+def blocks_kernel(x_ref, table_ref, out_ref, y_ref, out_sem):
     blocks = table_ref.shape[0]
     per = x_ref.shape[0] // blocks
     table = table_ref[...]
@@ -119,13 +123,17 @@
         hi, mid, lo = split3(x)
         y = dot_nn(table, hi) + dot_nn(table, mid) + dot_nn(table, lo)
         for i in range(2):
-            part = y[:, i * LANES : (i + 1) * LANES]
-            y_ref[pl.ds(j + i, blocks, stride=per), :] = part
-            turned_ref[pl.ds((j + i) * LANES, LANES), :] = part.T
+            y_ref[pl.ds(j + i, blocks, stride=per), :] = y[:, i * LANES : (i + 1) * LANES]
     out = pltpu.make_async_copy(y_ref, out_ref, out_sem)
     out.start()
+    out.wait()
+
+
+def gram_kernel(width, blocks, y_ref, hits_ref, packed_ref, turned_ref):
+    per = y_ref.shape[0] // blocks
+    for j in range(per):
+        turned_ref[pl.ds(j * LANES, LANES), :] = y_ref[pl.ds(j, blocks, stride=per), :].T
     gram_terms(width, turned_ref, hits_ref, packed_ref)
-    out.wait()
 
 
 def hits_kernel(local_bits, me_ref, sampled_ref, out_ref):
@@ -172,9 +180,15 @@
         at += width - i
 
 
-def factor_kernel(x_ref, partner_ref, gram_ref, factor_ref, full_ref):
+def copies_kernel(x_ref, one_ref, two_ref, three_ref, out_ref):
+    total = (x_ref[...] + one_ref[...]) + (two_ref[...] + three_ref[...])
+    for k in range(out_ref.shape[0]):
+        out_ref[k] = total
+
+
+def factor_kernel(x_ref, gram_ref, factor_ref, full_ref):
     width = gram_ref.shape[0]
-    packed = (x_ref[...] + partner_ref[...]) / jnp.float32(SAMPLES)
+    packed = x_ref[...] / jnp.float32(SAMPLES)
     full_ref[...] = jnp.zeros_like(full_ref)
     at = 0
     for i in range(0, width, PACK):
@@ -243,19 +257,25 @@
     return x.reshape(shape)
 
 
-def sum_over(x, axis):
-    count = lax.axis_size(axis)
-    x = jnp.broadcast_to(x[None], (count,) + x.shape)
-    return jnp.sum(lax.all_to_all(x, axis, 0, 0, tiled=True), axis=0)
-
-
-def sum_pairwise(x, axis):
-    count = lax.axis_size(axis)
-    partner = jnp.zeros_like(x)
-    for bit in range(count.bit_length() - 1):
-        x = x + partner if bit else x
-        partner = lax.ppermute(x, axis, [(i, i ^ 1 << bit) for i in range(count)])
-    return x, partner
+def sum_over(x, bits):
+    total = lax.axis_size(AXES)
+    member = [sum((k >> n & 1) << bit for n, bit in enumerate(bits)) for k in range(1 << len(bits))]
+    groups = [[i | m for m in member] for i in range(total) if not i & member[-1]]
+    return jnp.sum(lax.all_to_all(x, AXES, 0, 0, tiled=True, axis_index_groups=groups), axis=0)
+
+
+def sum_pairwise(x, bits):
+    for bit in bits:
+        x = x + from_partner(x, 1 << bit)
+    return x
+
+
+def from_others(x, bits):
+    return [from_partner(x, apart) for apart in (1 << bits[0], 1 << bits[1], 1 << bits[0] | 1 << bits[1])]
+
+
+def from_partner(x, apart):
+    return lax.ppermute(x, AXES, [(i, i ^ apart) for i in range(lax.axis_size(AXES))])
 
 
 def per_device(slab, flips, sampled):
@@ -270,8 +290,8 @@
     (local,) = call(
         lambda *refs: local_kernel(scale, *refs),
         [(lines, LANES)],
-        slab,
-        flips.reshape(outer, LANES),
+        pltpu.with_memory_space_constraint(slab, pltpu.HBM),
+        pltpu.with_memory_space_constraint(flips.reshape(outer, LANES), pltpu.HBM),
         specs=[HBM, HBM],
         out_specs=[HBM],
         scratch=[
@@ -293,18 +313,37 @@
         specs=[SMEM, VMEM],
         name="sampled_hits",
     )
-    whole, partial = call(
-        lambda *refs: blocks_kernel(width, *refs),
-        [(lines, LANES), (PACK, LANES)],
+    there, hits = lax.optimization_barrier((there, hits))
+    (whole,) = call(
+        blocks_kernel,
+        [(lines, LANES)],
         there,
         jnp.asarray(walsh(blocks)),
+        out_specs=[HBM],
+        scratch=[pltpu.VMEM((lines, LANES), jnp.float32), dma],
+        name="block_transform",
+    )
+    back = exchange(whole, blocks)
+    (partial,) = call(
+        lambda *refs: gram_kernel(width, blocks, *refs),
+        [(PACK, LANES)],
+        whole,
         hits,
-        out_specs=[HBM, VMEM],
-        scratch=[pltpu.VMEM((lines, LANES), jnp.float32), pltpu.VMEM((width * A_LO, blocks), jnp.float32), dma],
-        name="block_transform",
-    )
-    whole, partial = lax.optimization_barrier((whole, sum_over(partial, "group")))
-    back = exchange(whole, blocks)
+        scratch=[pltpu.VMEM((width * A_LO, blocks), jnp.float32)],
+        name="gram_terms",
+    )
+    partial = sum_pairwise(partial, NEAR)
+    one, two, three = from_others(partial, MIDDLE)
+    partial = (partial + one) + (two + three)
+    (partial,) = call(
+        copies_kernel,
+        [(1 << len(FAR), PACK, LANES)],
+        partial,
+        *from_others(partial, LAST),
+        name="gram_copies",
+    )
+    back, partial = lax.optimization_barrier((back, partial))
+    total = sum_over(partial, FAR)
     (mixed,) = call(
         lambda *refs: turn_kernel(width, *refs),
         [(width, rows)],
@@ -316,7 +355,7 @@
     gram, factor = call(
         factor_kernel,
         [(width, width)] * 2,
-        *sum_pairwise(partial, "dev"),
+        total,
         scratch=[pltpu.VMEM((width, LANES), jnp.float32)],
         name="factor",
     )

time: 143 us -> 140 us (0.979)
  starting transfers between devices: 47.7 us -> 61.5 us
  blocking collectives: 11.7 us -> 0 us
  waiting for transfers between devices: 69.4 us -> 63.8 us
  Pallas kernels: 10.4 us -> 13.6 us
  local copies, waits for them, and re-layouts: 2.18 us -> 0.01 us
    ppermute x5 -> x7, waiting for transfers between devices: 20.7 us -> 5.97 us  [from_partner(): lax.ppermute(x, AXES, [(i, i ^ apart) for i in range(lax.axis_size(AXES))])]
    ppermute x5 -> x7, starting transfers between devices: 15 us -> 26.7 us  [from_partner(): lax.ppermute(x, AXES, [(i, i ^ apart) for i in range(lax.axis_size(AXES))])]
    all_to_all x1 -> x0, blocking collectives: 11.7 us -> none  [sum_over(): return jnp.sum(lax.all_to_all(x, axis, 0, 0, tiled=True), axis=0)]
    all_to_all x0 -> x1, waiting for transfers between devices: none -> 7.17 us  [sum_over(): lax.all_to_all(x, AXES, 0, 0, tiled=True, axis_index_groups=groups)]
    all_to_all x0 -> x1, starting transfers between devices: none -> 3.51 us  [sum_over(): lax.all_to_all(x, AXES, 0, 0, tiled=True, axis_index_groups=groups)]
    pallas_call x5 -> x7, Pallas kernels: 10.4 us -> 13.6 us  [call(): pl.pallas_call(kernel, out_shape=out, in_specs=specs or [VMEM] * len(oper...]
    unnamed x8 -> x4, local copies, waits for them, and re-layouts: 2.17 us -> 0.01 us
    all_to_all x2, waiting for transfers between devices: 48.8 us -> 50.6 us  [exchange(): lax.all_to_all(x.reshape(blocks, x.size // blocks), AXES, 0, 0, tiled=True)]
  transfers between devices with their start and end apart: 7 -> 10, of which waited for: 7 -> 6; matrix products, arithmetic and copies ran while one was open for 0% -> 0% of each run, Pallas kernels for 2% -> 4%
where the time goes in v3:
time: 140 us
  waiting for transfers between devices  63.8 us (46%)
  starting transfers between devices  61.5 us (44%)
  Pallas kernels  13.6 us (10%)
    all_to_all x2, waiting for transfers between devices, exchange(): lax.all_to_all(x.reshape(blocks, x.size // blocks), AXES, 0, 0, tiled=True)  50.6 us
    all_to_all x2, starting transfers between devices, exchange(): lax.all_to_all(x.reshape(blocks, x.size // blocks), AXES, 0, 0, tiled=True)  31.3 us
    ppermute x7, starting transfers between devices, from_partner(): lax.ppermute(x, AXES, [(i, i ^ apart) for i in range(lax.axis_size(AXES))])  26.7 us
    pallas_call x7, Pallas kernels, call(): pl.pallas_call(kernel, out_shape=out, in_specs=specs or [VMEM] * len(oper...  13.6 us
    all_to_all x1, waiting for transfers between devices, sum_over(): lax.all_to_all(x, AXES, 0, 0, tiled=True, axis_index_groups=groups)  7.17 us
    ppermute x7, waiting for transfers between devices, from_partner(): lax.ppermute(x, AXES, [(i, i ^ apart) for i in range(lax.axis_size(AXES))])  5.97 us
    all_to_all x1, starting transfers between devices, sum_over(): lax.all_to_all(x, AXES, 0, 0, tiled=True, axis_index_groups=groups)  3.51 us
  transfers between devices with their start and end apart: 10, of which 6 were waited for; matrix products, arithmetic and copies ran while one was open for 0% of the time, Pallas kernels for 4%

profile of v3, /device:TPU:1, one launch (start us, length us, event | category | flops | bytes accessed | tf_op | source)
XLA Modules:
  0.0 139.7 jit_solution(14844659369263435605)
XLA Ops:
  0.6 3.6 %local_transform.1 = f32[3072,128]{1,0:T(8,128)} custom-call(f32[48,8192]{1,0:T(8,128)} %refs_0_.1, s32[64,128]{1,0:T(8,128)} %bitcast.10), custom_call_target="tpu_custom_call" | custom-call | tf_op jit(solution)/shard_map/local_transform/pallas_call | solution.py:243
  4.2 0.0 copy-start.1
  4.2 0.0 copy-start
  4.2 22.2 %all-to-all-start = ((f32[512,1,768]{2,1,0:T(1,128)}), f32[512,1,768]{2,1,0:T(1,128)S(1)}, u32[]{:S(2)}, u32[]{:S(2)}) async-start(f32[512,1,768]{2,1,0:T(1,128)} %bitcast.1), calls=%async_computation | async-start | bytes 3145728 | tf_op jit(solution)/shard_map/all_to_all | solution.py:256
  26.4 0.0 copy-done.1
  26.4 1.2 sampled_hits.1.refs_1_
  27.6 42.6 %all-to-all-done = f32[512,1,768]{2,1,0:T(1,128)S(1)} async-done(((f32[512,1,768]{2,1,0:T(1,128)}), f32[512,1,768]{2,1,0:T(1,128)S(1)}, u32[]{:S(2)}, u32[]{:S(2)}) %all-to-all-start) | async-done | bytes 1572896 | tf_op jit(solution)/shard_map/all_to_all | solution.py:256
  70.3 0.0 copy-done
  70.3 2.6 %block_transform.1.refs_0_ = f32[3072,128]{1,0:T(8,128)} custom-call(f32[3072,128]{1,0:T(8,128)S(1)} %bitcast.8, bf16[512,512]{1,0:T(8,128)(2,1)S(1)} %copy-done), custom_call_target="tpu_custom_call" | custom-call | tf_op jit(solution)/shard_map/block_transform/pallas_call | solution.py:243
  72.9 9.1 %all-to-all-start.1 = ((f32[512,1,768]{2,1,0:T(1,128)}), f32[512,1,768]{2,1,0:T(1,128)S(1)}, u32[]{:S(2)}, u32[]{:S(2)}) async-start(f32[512,1,768]{2,1,0:T(1,128)} %bitcast.5), calls=%async_computation.1 | async-start | bytes 3145728 | tf_op jit(solution)/shard_map/all_to_all | solution.py:256
  82.0 2.5 %gram_terms.1 = f32[16,128]{1,0:T(8,128)S(1)} custom-call(f32[3072,128]{1,0:T(8,128)} %block_transform.1.refs_0_, f32[64,128]{1,0:T(8,128)S(1)} %sampled_hits.1.refs_1_), custom_call_target="tpu_custom_call" | custom-call | tf_op jit(solution)/shard_map/gram_terms/pallas_call | solution.py:243
  84.5 6.2 %collective-permute-start = (f32[16,128]{1,0:T(8,128)S(1)}, f32[16,128]{1,0:T(8,128)S(1)}, u32[]{:S(2)}, u32[]{:S(2)}) collective-permute-start(f32[16,128]{1,0:T(8,128)S(1)} %gram_terms.1), channel_id=1, source_target_pairs={{0,1},{1,0},{2,3},{3,2},{4,5},{5,4},{6,7},{7,6},{8,9},{9,8},{10,11... | collective-permute-start | bytes 24584 | tf_op jit(solution)/shard_map/ppermute | solution.py:278
  90.7 0.8 collective-permute-done
  91.5 1.9 %collective-permute-start.3 = (f32[16,128]{1,0:T(8,128)S(1)}, f32[16,128]{1,0:T(8,128)S(1)}, u32[]{:S(2)}, u32[]{:S(2)}) collective-permute-start(f32[16,128]{1,0:T(8,128)S(1)} %add.16), channel_id=1, source_target_pairs={{0,6},{1,7},{2,4},{3,5},{4,2},{5,3},{6,0},{7,1},{8,14},{9,15},{10,... | collective-permute-start | bytes 24584 | tf_op jit(solution)/shard_map/ppermute | solution.py:278
  93.4 1.9 %collective-permute-start.2 = (f32[16,128]{1,0:T(8,128)S(1)}, f32[16,128]{1,0:T(8,128)S(1)}, u32[]{:S(2)}, u32[]{:S(2)}) collective-permute-start(f32[16,128]{1,0:T(8,128)S(1)} %add.16), channel_id=1, source_target_pairs={{0,4},{1,5},{2,6},{3,7},{4,0},{5,1},{6,2},{7,3},{8,12},{9,13},{10,... | collective-permute-start | bytes 24584 | tf_op jit(solution)/shard_map/ppermute | solution.py:278
  95.4 5.1 %collective-permute-start.1 = (f32[16,128]{1,0:T(8,128)S(1)}, f32[16,128]{1,0:T(8,128)S(1)}, u32[]{:S(2)}, u32[]{:S(2)}) collective-permute-start(f32[16,128]{1,0:T(8,128)S(1)} %add.16), channel_id=1, source_target_pairs={{0,2},{1,3},{2,0},{3,1},{4,6},{5,7},{6,4},{7,5},{8,10},{9,11},{10,... | collective-permute-start | bytes 24584 | tf_op jit(solution)/shard_map/ppermute | solution.py:278
  100.5 0.0 collective-permute-done.3
  100.5 0.0 collective-permute-done.2
  100.5 1.5 %collective-permute-done.1 = f32[16,128]{1,0:T(8,128)S(1)} collective-permute-done((f32[16,128]{1,0:T(8,128)S(1)}, f32[16,128]{1,0:T(8,128)S(1)}, u32[]{:S(2)}, u32[]{:S(2)}) %collective-permute-start.1) | collective-permute-done | bytes 8224 | tf_op jit(solution)/shard_map/ppermute | solution.py:278
  102.0 5.6 %collective-permute-start.6 = (f32[16,128]{1,0:T(8,128)S(1)}, f32[16,128]{1,0:T(8,128)S(1)}, u32[]{:S(2)}, u32[]{:S(2)}) collective-permute-start(f32[16,128]{1,0:T(8,128)S(1)} %add_add_fusion.x_ref), channel_id=1, source_target_pairs={{0,24},{1,25},{2,26},{3,27},{4,28},{5,29},{6,30},{7,31},{8,16},{9,... | collective-permute-start | bytes 24584 | tf_op jit(solution)/shard_map/ppermute | solution.py:278
  107.6 2.6 %collective-permute-start.5 = (f32[16,128]{1,0:T(8,128)S(1)}, f32[16,128]{1,0:T(8,128)S(1)}, u32[]{:S(2)}, u32[]{:S(2)}) collective-permute-start(f32[16,128]{1,0:T(8,128)S(1)} %add_add_fusion.x_ref), channel_id=1, source_target_pairs={{0,16},{1,17},{2,18},{3,19},{4,20},{5,21},{6,22},{7,23},{8,24},{9,... | collective-permute-start | bytes 24584 | tf_op jit(solution)/shard_map/ppermute | solution.py:278
  110.2 3.3 %collective-permute-start.4 = (f32[16,128]{1,0:T(8,128)S(1)}, f32[16,128]{1,0:T(8,128)S(1)}, u32[]{:S(2)}, u32[]{:S(2)}) collective-permute-start(f32[16,128]{1,0:T(8,128)S(1)} %add_add_fusion.x_ref), channel_id=1, source_target_pairs={{0,8},{1,9},{2,10},{3,11},{4,12},{5,13},{6,14},{7,15},{8,0},{9,1},... | collective-permute-start | bytes 24584 | tf_op jit(solution)/shard_map/ppermute | solution.py:278
  113.5 0.0 collective-permute-done.6.three_ref
  113.5 3.7 %collective-permute-done.5.two_ref = f32[16,128]{1,0:T(8,128)S(1)} collective-permute-done((f32[16,128]{1,0:T(8,128)S(1)}, f32[16,128]{1,0:T(8,128)S(1)}, u32[]{:S(2)}, u32[]{:S(2)}) %collective-permute-start.5) | collective-permute-done | bytes 8224 | tf_op jit(solution)/shard_map/ppermute | solution.py:278
  117.2 0.0 collective-permute-done.4.one_ref
  117.2 0.7 gram_copies.1
  117.9 8.0 %all-to-all-done.1 = f32[512,1,768]{2,1,0:T(1,128)S(1)} async-done(((f32[512,1,768]{2,1,0:T(1,128)}), f32[512,1,768]{2,1,0:T(1,128)S(1)}, u32[]{:S(2)}, u32[]{:S(2)}) %all-to-all-start.1) | async-done | bytes 1572896 | tf_op jit(solution)/shard_map/all_to_all | solution.py:256
  125.9 3.5 %all-to-all-start.2 = ((f32[16,16,128]{2,1,0:T(8,128)}), f32[16,16,128]{2,1,0:T(8,128)S(1)}, u32[]{:S(2)}, u32[]{:S(2)}) async-start(f32[16,16,128]{2,1,0:T(8,128)} %gram_copies.1), calls=%async_computation.2 | async-start | bytes 262144 | tf_op jit(solution)/shard_map/all_to_all | solution.py:264
  129.4 1.3 turn_back.1
  130.8 7.2 %all-to-all-done.2 = f32[16,16,128]{2,1,0:T(8,128)S(1)} async-done(((f32[16,16,128]{2,1,0:T(8,128)}), f32[16,16,128]{2,1,0:T(8,128)S(1)}, u32[]{:S(2)}, u32[]{:S(2)}) %all-to-all-start.2) | async-done | bytes 131104 | tf_op jit(solution)/shard_map/all_to_all | solution.py:264
  137.9 1.8 %factor.1 = (f32[48,48]{1,0:T(8,128)}, f32[48,48]{1,0:T(8,128)}) custom-call(f32[16,128]{1,0:T(8,128)S(1)} %reduce_sum.9.x_ref), custom_call_target="tpu_custom_call" | custom-call | tf_op jit(solution)/shard_map/factor/pallas_call | solution.py:243
  (3 shorter events, 0.0 us)
Async XLA Ops:
  4.2 22.2 %copy-start.1 = (s32[12288]{0:T(1024)S(1)}, s32[12288]{0:T(1024)}, u32[]{:S(2)}) copy-start(s32[12288]{0:T(1024)} %param.6) | copy-start | bytes 147460
  4.2 66.1 %copy-start = (bf16[512,512]{1,0:T(8,128)(2,1)S(1)}, bf16[512,512]{1,0:T(8,128)(2,1)}, u32[]{:S(2)}) copy-start(bf16[512,512]{1,0:T(8,128)(2,1)} %constant.15.clone.table_ref) | copy-start | bytes 1572868
  4.2 66.1 %all-to-all-start = ((f32[512,1,768]{2,1,0:T(1,128)}), f32[512,1,768]{2,1,0:T(1,128)S(1)}, u32[]{:S(2)}, u32[]{:S(2)}) async-start(f32[512,1,768]{2,1,0:T(1,128)} %bitcast.1), calls=%async_computation | async-start | bytes 3145728 | tf_op jit(solution)/shard_map/all_to_all | solution.py:256
  72.9 53.0 %all-to-all-start.1 = ((f32[512,1,768]{2,1,0:T(1,128)}), f32[512,1,768]{2,1,0:T(1,128)S(1)}, u32[]{:S(2)}, u32[]{:S(2)}) async-start(f32[512,1,768]{2,1,0:T(1,128)} %bitcast.5), calls=%async_computation.1 | async-start | bytes 3145728 | tf_op jit(solution)/shard_map/all_to_all | solution.py:256
  84.5 7.0 %collective-permute-start = (f32[16,128]{1,0:T(8,128)S(1)}, f32[16,128]{1,0:T(8,128)S(1)}, u32[]{:S(2)}, u32[]{:S(2)}) collective-permute-start(f32[16,128]{1,0:T(8,128)S(1)} %gram_terms.1), channel_id=1, source_target_pairs={{0,1},{1,0},{2,3},{3,2},{4,5},{5,4},{6,7},{7,6},{8,9},{9,8},{10,11... | collective-permute-start | bytes 24584 | tf_op jit(solution)/shard_map/ppermute | solution.py:278
  91.5 9.0 %collective-permute-start.3 = (f32[16,128]{1,0:T(8,128)S(1)}, f32[16,128]{1,0:T(8,128)S(1)}, u32[]{:S(2)}, u32[]{:S(2)}) collective-permute-start(f32[16,128]{1,0:T(8,128)S(1)} %add.16), channel_id=1, source_target_pairs={{0,6},{1,7},{2,4},{3,5},{4,2},{5,3},{6,0},{7,1},{8,14},{9,15},{10,... | collective-permute-start | bytes 24584 | tf_op jit(solution)/shard_map/ppermute | solution.py:278
  93.4 7.1 %collective-permute-start.2 = (f32[16,128]{1,0:T(8,128)S(1)}, f32[16,128]{1,0:T(8,128)S(1)}, u32[]{:S(2)}, u32[]{:S(2)}) collective-permute-start(f32[16,128]{1,0:T(8,128)S(1)} %add.16), channel_id=1, source_target_pairs={{0,4},{1,5},{2,6},{3,7},{4,0},{5,1},{6,2},{7,3},{8,12},{9,13},{10,... | collective-permute-start | bytes 24584 | tf_op jit(solution)/shard_map/ppermute | solution.py:278
  95.4 6.6 %collective-permute-start.1 = (f32[16,128]{1,0:T(8,128)S(1)}, f32[16,128]{1,0:T(8,128)S(1)}, u32[]{:S(2)}, u32[]{:S(2)}) collective-permute-start(f32[16,128]{1,0:T(8,128)S(1)} %add.16), channel_id=1, source_target_pairs={{0,2},{1,3},{2,0},{3,1},{4,6},{5,7},{6,4},{7,5},{8,10},{9,11},{10,... | collective-permute-start | bytes 24584 | tf_op jit(solution)/shard_map/ppermute | solution.py:278
  102.0 11.6 %collective-permute-start.6 = (f32[16,128]{1,0:T(8,128)S(1)}, f32[16,128]{1,0:T(8,128)S(1)}, u32[]{:S(2)}, u32[]{:S(2)}) collective-permute-start(f32[16,128]{1,0:T(8,128)S(1)} %add_add_fusion.x_ref), channel_id=1, source_target_pairs={{0,24},{1,25},{2,26},{3,27},{4,28},{5,29},{6,30},{7,31},{8,16},{9,... | collective-permute-start | bytes 24584 | tf_op jit(solution)/shard_map/ppermute | solution.py:278
  107.6 9.6 %collective-permute-start.5 = (f32[16,128]{1,0:T(8,128)S(1)}, f32[16,128]{1,0:T(8,128)S(1)}, u32[]{:S(2)}, u32[]{:S(2)}) collective-permute-start(f32[16,128]{1,0:T(8,128)S(1)} %add_add_fusion.x_ref), channel_id=1, source_target_pairs={{0,16},{1,17},{2,18},{3,19},{4,20},{5,21},{6,22},{7,23},{8,24},{9,... | collective-permute-start | bytes 24584 | tf_op jit(solution)/shard_map/ppermute | solution.py:278
  110.2 7.0 %collective-permute-start.4 = (f32[16,128]{1,0:T(8,128)S(1)}, f32[16,128]{1,0:T(8,128)S(1)}, u32[]{:S(2)}, u32[]{:S(2)}) collective-permute-start(f32[16,128]{1,0:T(8,128)S(1)} %add_add_fusion.x_ref), channel_id=1, source_target_pairs={{0,8},{1,9},{2,10},{3,11},{4,12},{5,13},{6,14},{7,15},{8,0},{9,1},... | collective-permute-start | bytes 24584 | tf_op jit(solution)/shard_map/ppermute | solution.py:278
  125.9 12.0 %all-to-all-start.2 = ((f32[16,16,128]{2,1,0:T(8,128)}), f32[16,16,128]{2,1,0:T(8,128)S(1)}, u32[]{:S(2)}, u32[]{:S(2)}) async-start(f32[16,16,128]{2,1,0:T(8,128)} %gram_copies.1), calls=%async_computation.2 | async-start | bytes 262144 | tf_op jit(solution)/shard_map/all_to_all | solution.py:264

commit v4 on v3

--- a/solution.py
+++ b/solution.py
@@ -2,7 +2,6 @@
 
 import jax
 import jax.numpy as jnp
-import numpy as np
 from jax import lax
 from jax.experimental import pallas as pl
 from jax.experimental.pallas import tpu as pltpu
@@ -23,15 +22,6 @@
 SMEM = pl.BlockSpec(memory_space=pltpu.SMEM)
 
 
-def walsh(length):
-    index = np.arange(length)
-    anded = index[:, None] & index[None, :]
-    parity = np.zeros((length, length), np.int32)
-    for bit in range(length.bit_length() - 1):
-        parity ^= anded >> bit & 1
-    return (1 - 2 * parity).astype(jnp.bfloat16)
-
-
 def split3(x):
     hi = x.astype(jnp.bfloat16)
     rest = x - hi.astype(jnp.float32)
@@ -44,18 +34,7 @@
     return lax.dot_general(x, y, (((1,), (1,)), ((), ())), preferred_element_type=jnp.float32)
 
 
-def dot_nn(x, y):
-    return lax.dot_general(x, y, (((1,), (0,)), ((), ())), preferred_element_type=jnp.float32)
-
-
-def walsh_in_kernel(shape):
-    anded = lax.broadcasted_iota(jnp.int32, shape, 0) & lax.broadcasted_iota(jnp.int32, shape, 1)
-    for shift in (4, 2, 1):
-        anded = anded ^ anded >> shift
-    return (1 - 2 * (anded & 1)).astype(jnp.float32).astype(jnp.bfloat16)
-
-
-def local_kernel(scale, slab_ref, flips_ref, out_ref, field_ref, signs_ref, turned_ref, in_sem, flip_sem, out_sem):
+def local_kernel(scale, slab_ref, flips_ref, out_ref, field_ref, signs_ref, turned_ref, done_ref, in_sem, flip_sem, out_sem):
     width, rows = slab_ref.shape
     outer = rows // LANES
     flips_in = pltpu.make_async_copy(flips_ref, signs_ref, flip_sem)
@@ -65,8 +44,6 @@
         part = pl.ds(tile * 8, 8)
         slab_in.append(pltpu.make_async_copy(slab_ref.at[part], field_ref.at[part], in_sem.at[tile]))
         slab_in[-1].start()
-    table = walsh_in_kernel((LANES, LANES))
-    table2 = jnp.concatenate([table, table], axis=1)
     flips_in.wait()
     signs = (1 - 2 * signs_ref[...]).astype(jnp.float32) * scale
     for tile in range(width // 8):
@@ -82,24 +59,35 @@
             for k in range(8):
                 a = k * (outer // 8) + first
                 field_ref[rows8, pl.ds(a * LANES, LANES)] = parts[k]
-        for first in range(0, outer, 8):
-            parts = [field_ref[rows8, pl.ds((first + k) * LANES, LANES)] for k in range(8)]
-            for half in (4, 2, 1):
-                parts = butterfly(parts, half)
-            for k in range(8):
-                field_ref[rows8, pl.ds((first + k) * LANES, LANES)] = parts[k]
     per = width * A_LO // LANES
     out = []
     for a_hi in range(outer // A_LO):
+        for first in range(a_hi * A_LO, (a_hi + 1) * A_LO, 8):
+            for tile in range(width // 8):
+                rows8 = pl.ds(tile * 8, 8)
+                parts = [field_ref[rows8, pl.ds((first + k) * LANES, LANES)] for k in range(8)]
+                for half in (4, 2, 1):
+                    parts = butterfly(parts, half)
+                for k in range(8):
+                    field_ref[rows8, pl.ds((first + k) * LANES, LANES)] = parts[k]
         block = jnp.concatenate(
             [field_ref[:, pl.ds((a_hi * A_LO + a) * LANES, LANES)] for a in range(A_LO)], axis=0
         )
-        hi, mid, lo = split3(block)
-        turned = dot_nt(table2, jnp.concatenate([hi, mid], axis=1)) + dot_nt(table, lo)
         for j in range(per):
-            turned_ref[pl.ds(a_hi * LANES * per + j, LANES, stride=per), :] = turned[:, j * LANES : (j + 1) * LANES]
+            start = (a_hi * per + j) * LANES
+            turned = block[j * LANES : (j + 1) * LANES, :].T
+            parts = [turned[k : k + 8, :] for k in range(0, LANES, 8)]
+            for half in (8, 4, 2, 1):
+                parts = butterfly(parts, half)
+            for k in range(LANES // 8):
+                turned_ref[pl.ds(start + 8 * k, 8), :] = parts[k]
+            parts = [turned_ref[pl.ds(start + k, LANES // 8, stride=8), :] for k in range(8)]
+            for half in (4, 2, 1):
+                parts = butterfly(parts, half)
+            for k in range(8):
+                done_ref[pl.ds((a_hi * LANES + k) * per + j, LANES // 8, stride=8 * per), :] = parts[k]
         part = pl.ds(a_hi * LANES * per, LANES * per)
-        out.append(pltpu.make_async_copy(turned_ref.at[part], out_ref.at[part], out_sem.at[a_hi]))
+        out.append(pltpu.make_async_copy(done_ref.at[part], out_ref.at[part], out_sem.at[a_hi]))
         out[-1].start()
     for copy in out:
         copy.wait()
@@ -114,19 +102,35 @@
     return out
 
 
-def blocks_kernel(x_ref, table_ref, out_ref, y_ref, out_sem):
-    blocks = table_ref.shape[0]
+def blocks_kernel(blocks, x_ref, out_ref, half_ref, y_ref, out_sem):
     per = x_ref.shape[0] // blocks
-    table = table_ref[...]
-    for j in range(0, per, 2):
-        x = jnp.concatenate([x_ref[pl.ds(j + i, blocks, stride=per), :] for i in range(2)], axis=1)
-        hi, mid, lo = split3(x)
-        y = dot_nn(table, hi) + dot_nn(table, mid) + dot_nn(table, lo)
-        for i in range(2):
-            y_ref[pl.ds(j + i, blocks, stride=per), :] = y[:, i * LANES : (i + 1) * LANES]
-    out = pltpu.make_async_copy(y_ref, out_ref, out_sem)
-    out.start()
-    out.wait()
+    far = blocks // 8
+    for j in range(per):
+        for first in range(0, far, 8):
+            parts = [x_ref[pl.ds((k * far + first) * per + j, 8, stride=per), :] for k in range(8)]
+            for half in (4, 2, 1):
+                parts = butterfly(parts, half)
+            for k in range(8):
+                half_ref[pl.ds(j * blocks + k * far + first, 8), :] = parts[k]
+    out = []
+    for first in range(0, blocks, 64):
+        for j in range(per):
+            start = j * blocks + first
+            parts = [half_ref[pl.ds(start + 8 * k, 8), :] for k in range(8)]
+            for half in (4, 2, 1):
+                parts = butterfly(parts, half)
+            for k in range(8):
+                half_ref[pl.ds(start + 8 * k, 8), :] = parts[k]
+            parts = [half_ref[pl.ds(start + k, 8, stride=8), :] for k in range(8)]
+            for half in (4, 2, 1):
+                parts = butterfly(parts, half)
+            for k in range(8):
+                y_ref[pl.ds((first + k) * per + j, 8, stride=8 * per), :] = parts[k]
+        part = pl.ds(first * per, 64 * per)
+        out.append(pltpu.make_async_copy(y_ref.at[part], out_ref.at[part], out_sem.at[first // 64]))
+        out[-1].start()
+    for copy in out:
+        copy.wait()
 
 
 def gram_kernel(width, blocks, y_ref, hits_ref, packed_ref, turned_ref):
@@ -298,6 +302,7 @@
             pltpu.VMEM((width, rows), jnp.float32),
             pltpu.VMEM((outer, LANES), jnp.int32),
             pltpu.VMEM((lines, LANES), jnp.float32),
+            pltpu.VMEM((lines, LANES), jnp.float32),
             dma((width // 8,)),
             dma,
             dma((outer // A_LO,)),
@@ -315,12 +320,11 @@
     )
     there, hits = lax.optimization_barrier((there, hits))
     (whole,) = call(
-        blocks_kernel,
+        lambda *refs: blocks_kernel(blocks, *refs),
         [(lines, LANES)],
         there,
-        jnp.asarray(walsh(blocks)),
         out_specs=[HBM],
-        scratch=[pltpu.VMEM((lines, LANES), jnp.float32), dma],
+        scratch=[pltpu.VMEM((lines, LANES), jnp.float32)] * 2 + [dma((blocks // 64,))],
         name="block_transform",
     )
     back = exchange(whole, blocks)

time: 140 us -> 140 us (level)
  no operation moved by 1% of the time
where the time goes in v4:
time: 140 us; the launch traced here: 139 us
  waiting for transfers between devices  63.7 us (46%)
  starting transfers between devices  61.6 us (44%)
  Pallas kernels  12.7 us (9%)
    all_to_all x2, waiting for transfers between devices, exchange(): lax.all_to_all(x.reshape(blocks, x.size // blocks), AXES, 0, 0, tiled=True)  50.9 us
    all_to_all x2, starting transfers between devices, exchange(): lax.all_to_all(x.reshape(blocks, x.size // blocks), AXES, 0, 0, tiled=True)  31.3 us
    ppermute x7, starting transfers between devices, from_partner(): lax.ppermute(x, AXES, [(i, i ^ apart) for i in range(lax.axis_size(AXES))])  26.7 us
    pallas_call x7, Pallas kernels, call(): pl.pallas_call(kernel, out_shape=out, in_specs=specs or [VMEM] * len(oper...  12.7 us
    all_to_all x1, waiting for transfers between devices, sum_over(): lax.all_to_all(x, AXES, 0, 0, tiled=True, axis_index_groups=groups)  7.17 us
    ppermute x7, waiting for transfers between devices, from_partner(): lax.ppermute(x, AXES, [(i, i ^ apart) for i in range(lax.axis_size(AXES))])  5.7 us
    all_to_all x1, starting transfers between devices, sum_over(): lax.all_to_all(x, AXES, 0, 0, tiled=True, axis_index_groups=groups)  3.51 us
  transfers between devices with their start and end apart: 10, of which 6 were waited for; matrix products, arithmetic and copies ran while one was open for 0% of the time, Pallas kernels for 4%

profile of v4, /device:TPU:1, one launch (start us, length us, event | category | flops | bytes accessed | tf_op | source)
XLA Modules:
  0.0 138.8 jit_solution(3083903967899143842)
XLA Ops:
  0.6 3.5 %local_transform.1 = f32[3072,128]{1,0:T(8,128)} custom-call(f32[48,8192]{1,0:T(8,128)} %refs_0_.1, s32[64,128]{1,0:T(8,128)} %bitcast.10), custom_call_target="tpu_custom_call" | custom-call | tf_op jit(solution)/shard_map/local_transform/pallas_call | solution.py:247
  4.1 0.0 copy-start
  4.1 22.2 %all-to-all-start = ((f32[512,1,768]{2,1,0:T(1,128)}), f32[512,1,768]{2,1,0:T(1,128)S(1)}, u32[]{:S(2)}, u32[]{:S(2)}) async-start(f32[512,1,768]{2,1,0:T(1,128)} %bitcast.1), calls=%async_computation | async-start | bytes 3145728 | tf_op jit(solution)/shard_map/all_to_all | solution.py:260
  26.3 0.0 copy-done
  26.3 1.2 sampled_hits.1.refs_1_
  27.5 42.6 %all-to-all-done = f32[512,1,768]{2,1,0:T(1,128)S(1)} async-done(((f32[512,1,768]{2,1,0:T(1,128)}), f32[512,1,768]{2,1,0:T(1,128)S(1)}, u32[]{:S(2)}, u32[]{:S(2)}) %all-to-all-start) | async-done | bytes 1572896 | tf_op jit(solution)/shard_map/all_to_all | solution.py:260
  70.2 1.8 %block_transform.1.refs_0_ = f32[3072,128]{1,0:T(8,128)} custom-call(f32[3072,128]{1,0:T(8,128)S(1)} %bitcast.8), custom_call_target="tpu_custom_call" | custom-call | tf_op jit(solution)/shard_map/block_transform/pallas_call | solution.py:247
  72.0 9.1 %all-to-all-start.1 = ((f32[512,1,768]{2,1,0:T(1,128)}), f32[512,1,768]{2,1,0:T(1,128)S(1)}, u32[]{:S(2)}, u32[]{:S(2)}) async-start(f32[512,1,768]{2,1,0:T(1,128)} %bitcast.5), calls=%async_computation.1 | async-start | bytes 3145728 | tf_op jit(solution)/shard_map/all_to_all | solution.py:260
  81.1 2.5 %gram_terms.1 = f32[16,128]{1,0:T(8,128)S(1)} custom-call(f32[3072,128]{1,0:T(8,128)} %block_transform.1.refs_0_, f32[64,128]{1,0:T(8,128)S(1)} %sampled_hits.1.refs_1_), custom_call_target="tpu_custom_call" | custom-call | tf_op jit(solution)/shard_map/gram_terms/pallas_call | solution.py:247
  83.6 6.2 %collective-permute-start = (f32[16,128]{1,0:T(8,128)S(1)}, f32[16,128]{1,0:T(8,128)S(1)}, u32[]{:S(2)}, u32[]{:S(2)}) collective-permute-start(f32[16,128]{1,0:T(8,128)S(1)} %gram_terms.1), channel_id=1, source_target_pairs={{0,1},{1,0},{2,3},{3,2},{4,5},{5,4},{6,7},{7,6},{8,9},{9,8},{10,11... | collective-permute-start | bytes 24584 | tf_op jit(solution)/shard_map/ppermute | solution.py:282
  89.8 0.8 collective-permute-done
  90.6 1.9 %collective-permute-start.3 = (f32[16,128]{1,0:T(8,128)S(1)}, f32[16,128]{1,0:T(8,128)S(1)}, u32[]{:S(2)}, u32[]{:S(2)}) collective-permute-start(f32[16,128]{1,0:T(8,128)S(1)} %add.16), channel_id=1, source_target_pairs={{0,6},{1,7},{2,4},{3,5},{4,2},{5,3},{6,0},{7,1},{8,14},{9,15},{10,... | collective-permute-start | bytes 24584 | tf_op jit(solution)/shard_map/ppermute | solution.py:282
  92.5 1.9 %collective-permute-start.2 = (f32[16,128]{1,0:T(8,128)S(1)}, f32[16,128]{1,0:T(8,128)S(1)}, u32[]{:S(2)}, u32[]{:S(2)}) collective-permute-start(f32[16,128]{1,0:T(8,128)S(1)} %add.16), channel_id=1, source_target_pairs={{0,4},{1,5},{2,6},{3,7},{4,0},{5,1},{6,2},{7,3},{8,12},{9,13},{10,... | collective-permute-start | bytes 24584 | tf_op jit(solution)/shard_map/ppermute | solution.py:282
  94.5 5.1 %collective-permute-start.1 = (f32[16,128]{1,0:T(8,128)S(1)}, f32[16,128]{1,0:T(8,128)S(1)}, u32[]{:S(2)}, u32[]{:S(2)}) collective-permute-start(f32[16,128]{1,0:T(8,128)S(1)} %add.16), channel_id=1, source_target_pairs={{0,2},{1,3},{2,0},{3,1},{4,6},{5,7},{6,4},{7,5},{8,10},{9,11},{10,... | collective-permute-start | bytes 24584 | tf_op jit(solution)/shard_map/ppermute | solution.py:282
  99.6 0.0 collective-permute-done.3
  99.6 0.0 collective-permute-done.2
  99.6 1.4 %collective-permute-done.1 = f32[16,128]{1,0:T(8,128)S(1)} collective-permute-done((f32[16,128]{1,0:T(8,128)S(1)}, f32[16,128]{1,0:T(8,128)S(1)}, u32[]{:S(2)}, u32[]{:S(2)}) %collective-permute-start.1) | collective-permute-done | bytes 8224 | tf_op jit(solution)/shard_map/ppermute | solution.py:282
  101.0 5.7 %collective-permute-start.6 = (f32[16,128]{1,0:T(8,128)S(1)}, f32[16,128]{1,0:T(8,128)S(1)}, u32[]{:S(2)}, u32[]{:S(2)}) collective-permute-start(f32[16,128]{1,0:T(8,128)S(1)} %add_add_fusion.x_ref), channel_id=1, source_target_pairs={{0,24},{1,25},{2,26},{3,27},{4,28},{5,29},{6,30},{7,31},{8,16},{9,... | collective-permute-start | bytes 24584 | tf_op jit(solution)/shard_map/ppermute | solution.py:282
  106.7 2.6 %collective-permute-start.5 = (f32[16,128]{1,0:T(8,128)S(1)}, f32[16,128]{1,0:T(8,128)S(1)}, u32[]{:S(2)}, u32[]{:S(2)}) collective-permute-start(f32[16,128]{1,0:T(8,128)S(1)} %add_add_fusion.x_ref), channel_id=1, source_target_pairs={{0,16},{1,17},{2,18},{3,19},{4,20},{5,21},{6,22},{7,23},{8,24},{9,... | collective-permute-start | bytes 24584 | tf_op jit(solution)/shard_map/ppermute | solution.py:282
  109.3 3.3 %collective-permute-start.4 = (f32[16,128]{1,0:T(8,128)S(1)}, f32[16,128]{1,0:T(8,128)S(1)}, u32[]{:S(2)}, u32[]{:S(2)}) collective-permute-start(f32[16,128]{1,0:T(8,128)S(1)} %add_add_fusion.x_ref), channel_id=1, source_target_pairs={{0,8},{1,9},{2,10},{3,11},{4,12},{5,13},{6,14},{7,15},{8,0},{9,1},... | collective-permute-start | bytes 24584 | tf_op jit(solution)/shard_map/ppermute | solution.py:282
  112.6 0.0 collective-permute-done.6.three_ref
  112.6 3.5 %collective-permute-done.5.two_ref = f32[16,128]{1,0:T(8,128)S(1)} collective-permute-done((f32[16,128]{1,0:T(8,128)S(1)}, f32[16,128]{1,0:T(8,128)S(1)}, u32[]{:S(2)}, u32[]{:S(2)}) %collective-permute-start.5) | collective-permute-done | bytes 8224 | tf_op jit(solution)/shard_map/ppermute | solution.py:282
  116.1 0.0 collective-permute-done.4.one_ref
  116.1 0.7 gram_copies.1
  116.8 8.2 %all-to-all-done.1 = f32[512,1,768]{2,1,0:T(1,128)S(1)} async-done(((f32[512,1,768]{2,1,0:T(1,128)}), f32[512,1,768]{2,1,0:T(1,128)S(1)}, u32[]{:S(2)}, u32[]{:S(2)}) %all-to-all-start.1) | async-done | bytes 1572896 | tf_op jit(solution)/shard_map/all_to_all | solution.py:260
  125.0 3.5 %all-to-all-start.2 = ((f32[16,16,128]{2,1,0:T(8,128)}), f32[16,16,128]{2,1,0:T(8,128)S(1)}, u32[]{:S(2)}, u32[]{:S(2)}) async-start(f32[16,16,128]{2,1,0:T(8,128)} %gram_copies.1), calls=%async_computation.2 | async-start | bytes 262144 | tf_op jit(solution)/shard_map/all_to_all | solution.py:268
  128.5 1.3 turn_back.1
  129.9 7.2 %all-to-all-done.2 = f32[16,16,128]{2,1,0:T(8,128)S(1)} async-done(((f32[16,16,128]{2,1,0:T(8,128)}), f32[16,16,128]{2,1,0:T(8,128)S(1)}, u32[]{:S(2)}, u32[]{:S(2)}) %all-to-all-start.2) | async-done | bytes 131104 | tf_op jit(solution)/shard_map/all_to_all | solution.py:268
  137.0 1.8 %factor.1 = (f32[48,48]{1,0:T(8,128)}, f32[48,48]{1,0:T(8,128)}) custom-call(f32[16,128]{1,0:T(8,128)S(1)} %reduce_sum.9.x_ref), custom_call_target="tpu_custom_call" | custom-call | tf_op jit(solution)/shard_map/factor/pallas_call | solution.py:247
  (3 shorter events, 0.0 us)
Async XLA Ops:
  4.1 22.2 %copy-start = (s32[12288]{0:T(1024)S(1)}, s32[12288]{0:T(1024)}, u32[]{:S(2)}) copy-start(s32[12288]{0:T(1024)} %param.5) | copy-start | bytes 147460
  4.1 66.1 %all-to-all-start = ((f32[512,1,768]{2,1,0:T(1,128)}), f32[512,1,768]{2,1,0:T(1,128)S(1)}, u32[]{:S(2)}, u32[]{:S(2)}) async-start(f32[512,1,768]{2,1,0:T(1,128)} %bitcast.1), calls=%async_computation | async-start | bytes 3145728 | tf_op jit(solution)/shard_map/all_to_all | solution.py:260
  72.0 53.0 %all-to-all-start.1 = ((f32[512,1,768]{2,1,0:T(1,128)}), f32[512,1,768]{2,1,0:T(1,128)S(1)}, u32[]{:S(2)}, u32[]{:S(2)}) async-start(f32[512,1,768]{2,1,0:T(1,128)} %bitcast.5), calls=%async_computation.1 | async-start | bytes 3145728 | tf_op jit(solution)/shard_map/all_to_all | solution.py:260
  83.6 7.0 %collective-permute-start = (f32[16,128]{1,0:T(8,128)S(1)}, f32[16,128]{1,0:T(8,128)S(1)}, u32[]{:S(2)}, u32[]{:S(2)}) collective-permute-start(f32[16,128]{1,0:T(8,128)S(1)} %gram_terms.1), channel_id=1, source_target_pairs={{0,1},{1,0},{2,3},{3,2},{4,5},{5,4},{6,7},{7,6},{8,9},{9,8},{10,11... | collective-permute-start | bytes 24584 | tf_op jit(solution)/shard_map/ppermute | solution.py:282
  90.6 9.0 %collective-permute-start.3 = (f32[16,128]{1,0:T(8,128)S(1)}, f32[16,128]{1,0:T(8,128)S(1)}, u32[]{:S(2)}, u32[]{:S(2)}) collective-permute-start(f32[16,128]{1,0:T(8,128)S(1)} %add.16), channel_id=1, source_target_pairs={{0,6},{1,7},{2,4},{3,5},{4,2},{5,3},{6,0},{7,1},{8,14},{9,15},{10,... | collective-permute-start | bytes 24584 | tf_op jit(solution)/shard_map/ppermute | solution.py:282
  92.5 7.1 %collective-permute-start.2 = (f32[16,128]{1,0:T(8,128)S(1)}, f32[16,128]{1,0:T(8,128)S(1)}, u32[]{:S(2)}, u32[]{:S(2)}) collective-permute-start(f32[16,128]{1,0:T(8,128)S(1)} %add.16), channel_id=1, source_target_pairs={{0,4},{1,5},{2,6},{3,7},{4,0},{5,1},{6,2},{7,3},{8,12},{9,13},{10,... | collective-permute-start | bytes 24584 | tf_op jit(solution)/shard_map/ppermute | solution.py:282
  94.5 6.6 %collective-permute-start.1 = (f32[16,128]{1,0:T(8,128)S(1)}, f32[16,128]{1,0:T(8,128)S(1)}, u32[]{:S(2)}, u32[]{:S(2)}) collective-permute-start(f32[16,128]{1,0:T(8,128)S(1)} %add.16), channel_id=1, source_target_pairs={{0,2},{1,3},{2,0},{3,1},{4,6},{5,7},{6,4},{7,5},{8,10},{9,11},{10,... | collective-permute-start | bytes 24584 | tf_op jit(solution)/shard_map/ppermute | solution.py:282
  101.0 11.6 %collective-permute-start.6 = (f32[16,128]{1,0:T(8,128)S(1)}, f32[16,128]{1,0:T(8,128)S(1)}, u32[]{:S(2)}, u32[]{:S(2)}) collective-permute-start(f32[16,128]{1,0:T(8,128)S(1)} %add_add_fusion.x_ref), channel_id=1, source_target_pairs={{0,24},{1,25},{2,26},{3,27},{4,28},{5,29},{6,30},{7,31},{8,16},{9,... | collective-permute-start | bytes 24584 | tf_op jit(solution)/shard_map/ppermute | solution.py:282
  106.7 9.4 %collective-permute-start.5 = (f32[16,128]{1,0:T(8,128)S(1)}, f32[16,128]{1,0:T(8,128)S(1)}, u32[]{:S(2)}, u32[]{:S(2)}) collective-permute-start(f32[16,128]{1,0:T(8,128)S(1)} %add_add_fusion.x_ref), channel_id=1, source_target_pairs={{0,16},{1,17},{2,18},{3,19},{4,20},{5,21},{6,22},{7,23},{8,24},{9,... | collective-permute-start | bytes 24584 | tf_op jit(solution)/shard_map/ppermute | solution.py:282
  109.3 6.8 %collective-permute-start.4 = (f32[16,128]{1,0:T(8,128)S(1)}, f32[16,128]{1,0:T(8,128)S(1)}, u32[]{:S(2)}, u32[]{:S(2)}) collective-permute-start(f32[16,128]{1,0:T(8,128)S(1)} %add_add_fusion.x_ref), channel_id=1, source_target_pairs={{0,8},{1,9},{2,10},{3,11},{4,12},{5,13},{6,14},{7,15},{8,0},{9,1},... | collective-permute-start | bytes 24584 | tf_op jit(solution)/shard_map/ppermute | solution.py:282
  125.0 12.0 %all-to-all-start.2 = ((f32[16,16,128]{2,1,0:T(8,128)}), f32[16,16,128]{2,1,0:T(8,128)S(1)}, u32[]{:S(2)}, u32[]{:S(2)}) async-start(f32[16,16,128]{2,1,0:T(8,128)} %gram_copies.1), calls=%async_computation.2 | async-start | bytes 262144 | tf_op jit(solution)/shard_map/all_to_all | solution.py:268

commit v5 on v4

--- a/solution.py
+++ b/solution.py
@@ -12,6 +12,7 @@
 LANES = 128
 A_LO = 16
 PACK = 16
+DENSE = 12
 FAR = (5, 6, 7, 8)
 NEAR = (0,)
 MIDDLE = (1, 2)
@@ -184,15 +185,27 @@
         at += width - i
 
 
-def copies_kernel(x_ref, one_ref, two_ref, three_ref, out_ref):
+def copies_kernel(x_ref, one_ref, two_ref, three_ref, out_ref, dense_ref):
     total = (x_ref[...] + one_ref[...]) + (two_ref[...] + three_ref[...])
-    for k in range(out_ref.shape[0]):
-        out_ref[k] = total
-
-
-def factor_kernel(x_ref, gram_ref, factor_ref, full_ref):
+    dense_ref[...] = total[:DENSE, :]
+    for i in range(DENSE):
+        row, at = DENSE + i // 3, i % 3 * 32
+        dense_ref[pl.ds(i, 1), pl.ds(LANES - 32, 32)] = total[row : row + 1, at : at + 32]
+    dense = dense_ref[...]
+    for k in range(out_ref.shape[0] // DENSE):
+        out_ref[pl.ds(k * DENSE, DENSE), :] = dense
+
+
+def factor_kernel(x_ref, gram_ref, factor_ref, full_ref, packed_ref):
     width = gram_ref.shape[0]
-    packed = x_ref[...] / jnp.float32(SAMPLES)
+    total = x_ref[pl.ds(0, DENSE), :]
+    for k in range(1, x_ref.shape[0] // DENSE):
+        total = total + x_ref[pl.ds(k * DENSE, DENSE), :]
+    total = total / jnp.float32(SAMPLES)
+    packed_ref[pl.ds(0, DENSE), :] = total
+    for i in range(DENSE):
+        packed_ref[pl.ds(DENSE + i // 3, 1), pl.ds(i % 3 * 32, 32)] = total[i : i + 1, LANES - 32 :]
+    packed = packed_ref[...]
     full_ref[...] = jnp.zeros_like(full_ref)
     at = 0
     for i in range(0, width, PACK):
@@ -261,11 +274,12 @@
     return x.reshape(shape)
 
 
-def sum_over(x, bits):
+def from_all(x, bits):
     total = lax.axis_size(AXES)
     member = [sum((k >> n & 1) << bit for n, bit in enumerate(bits)) for k in range(1 << len(bits))]
     groups = [[i | m for m in member] for i in range(total) if not i & member[-1]]
-    return jnp.sum(lax.all_to_all(x, AXES, 0, 0, tiled=True, axis_index_groups=groups), axis=0)
+    parts = x.reshape(len(member), x.size // len(member))
+    return lax.all_to_all(parts, AXES, 0, 0, tiled=True, axis_index_groups=groups).reshape(x.shape)
 
 
 def sum_pairwise(x, bits):
@@ -341,13 +355,14 @@
     partial = (partial + one) + (two + three)
     (partial,) = call(
         copies_kernel,
-        [(1 << len(FAR), PACK, LANES)],
+        [(DENSE << len(FAR), LANES)],
         partial,
         *from_others(partial, LAST),
+        scratch=[pltpu.VMEM((DENSE, LANES), jnp.float32)],
         name="gram_copies",
     )
     back, partial = lax.optimization_barrier((back, partial))
-    total = sum_over(partial, FAR)
+    total = from_all(partial, FAR)
     (mixed,) = call(
         lambda *refs: turn_kernel(width, *refs),
         [(width, rows)],
@@ -360,7 +375,7 @@
         factor_kernel,
         [(width, width)] * 2,
         total,
-        scratch=[pltpu.VMEM((width, LANES), jnp.float32)],
+        scratch=[pltpu.VMEM((width, LANES), jnp.float32), pltpu.VMEM((PACK, LANES), jnp.float32)],
         name="factor",
     )
     return (mixed, gram, factor)

time: 140 us -> 139 us (level)
  no operation moved by 1% of the time
where the time goes in v5:
time: 139 us
  waiting for transfers between devices  63.4 us (46%)
  starting transfers between devices  61.6 us (44%)
  Pallas kernels  12.9 us (9%)
    all_to_all x2, waiting for transfers between devices, exchange(): lax.all_to_all(x.reshape(blocks, x.size // blocks), AXES, 0, 0, tiled=True)  50.8 us
    all_to_all x2, starting transfers between devices, exchange(): lax.all_to_all(x.reshape(blocks, x.size // blocks), AXES, 0, 0, tiled=True)  31.3 us
    ppermute x7, starting transfers between devices, from_partner(): lax.ppermute(x, AXES, [(i, i ^ apart) for i in range(lax.axis_size(AXES))])  26.7 us
    pallas_call x7, Pallas kernels, call(): pl.pallas_call(kernel, out_shape=out, in_specs=specs or [VMEM] * len(oper...  12.9 us
    all_to_all x1, waiting for transfers between devices, from_all(): lax.all_to_all(parts, AXES, 0, 0, tiled=True, axis_index_groups=groups)  6.91 us
    ppermute x7, waiting for transfers between devices, from_partner(): lax.ppermute(x, AXES, [(i, i ^ apart) for i in range(lax.axis_size(AXES))])  5.7 us
    all_to_all x1, starting transfers between devices, from_all(): lax.all_to_all(parts, AXES, 0, 0, tiled=True, axis_index_groups=groups)  3.51 us
  transfers between devices with their start and end apart: 10, of which 6 were waited for; matrix products, arithmetic and copies ran while one was open for 0% of the time, Pallas kernels for 4%

profile of v5, /device:TPU:1, one launch (start us, length us, event | category | flops | bytes accessed | tf_op | source)
XLA Modules:
  0.0 138.6 jit_solution(4392141621090791042)
XLA Ops:
  0.6 3.5 %local_transform.1 = f32[3072,128]{1,0:T(8,128)} custom-call(f32[48,8192]{1,0:T(8,128)} %refs_0_.1, s32[64,128]{1,0:T(8,128)} %bitcast.13), custom_call_target="tpu_custom_call" | custom-call | tf_op jit(solution)/shard_map/local_transform/pallas_call | solution.py:260
  4.1 0.0 copy-start
  4.1 22.2 %all-to-all-start = ((f32[512,1,768]{2,1,0:T(1,128)}), f32[512,1,768]{2,1,0:T(1,128)S(1)}, u32[]{:S(2)}, u32[]{:S(2)}) async-start(f32[512,1,768]{2,1,0:T(1,128)} %bitcast.1), calls=%async_computation | async-start | bytes 3145728 | tf_op jit(solution)/shard_map/all_to_all | solution.py:273
  26.3 0.0 copy-done
  26.3 1.2 sampled_hits.1.refs_1_
  27.5 42.6 %all-to-all-done = f32[512,1,768]{2,1,0:T(1,128)S(1)} async-done(((f32[512,1,768]{2,1,0:T(1,128)}), f32[512,1,768]{2,1,0:T(1,128)S(1)}, u32[]{:S(2)}, u32[]{:S(2)}) %all-to-all-start) | async-done | bytes 1572896 | tf_op jit(solution)/shard_map/all_to_all | solution.py:273
  70.2 1.8 %block_transform.1.refs_0_ = f32[3072,128]{1,0:T(8,128)} custom-call(f32[3072,128]{1,0:T(8,128)S(1)} %bitcast.10), custom_call_target="tpu_custom_call" | custom-call | tf_op jit(solution)/shard_map/block_transform/pallas_call | solution.py:260
  72.0 9.1 %all-to-all-start.1 = ((f32[512,1,768]{2,1,0:T(1,128)}), f32[512,1,768]{2,1,0:T(1,128)S(1)}, u32[]{:S(2)}, u32[]{:S(2)}) async-start(f32[512,1,768]{2,1,0:T(1,128)} %bitcast.5), calls=%async_computation.1 | async-start | bytes 3145728 | tf_op jit(solution)/shard_map/all_to_all | solution.py:273
  81.1 2.5 %gram_terms.1 = f32[16,128]{1,0:T(8,128)S(1)} custom-call(f32[3072,128]{1,0:T(8,128)} %block_transform.1.refs_0_, f32[64,128]{1,0:T(8,128)S(1)} %sampled_hits.1.refs_1_), custom_call_target="tpu_custom_call" | custom-call | tf_op jit(solution)/shard_map/gram_terms/pallas_call | solution.py:260
  83.6 6.2 %collective-permute-start = (f32[16,128]{1,0:T(8,128)S(1)}, f32[16,128]{1,0:T(8,128)S(1)}, u32[]{:S(2)}, u32[]{:S(2)}) collective-permute-start(f32[16,128]{1,0:T(8,128)S(1)} %gram_terms.1), channel_id=1, source_target_pairs={{0,1},{1,0},{2,3},{3,2},{4,5},{5,4},{6,7},{7,6},{8,9},{9,8},{10,11... | collective-permute-start | bytes 24584 | tf_op jit(solution)/shard_map/ppermute | solution.py:296
  89.8 0.8 collective-permute-done
  90.6 1.9 %collective-permute-start.3 = (f32[16,128]{1,0:T(8,128)S(1)}, f32[16,128]{1,0:T(8,128)S(1)}, u32[]{:S(2)}, u32[]{:S(2)}) collective-permute-start(f32[16,128]{1,0:T(8,128)S(1)} %add.16), channel_id=1, source_target_pairs={{0,6},{1,7},{2,4},{3,5},{4,2},{5,3},{6,0},{7,1},{8,14},{9,15},{10,... | collective-permute-start | bytes 24584 | tf_op jit(solution)/shard_map/ppermute | solution.py:296
  92.5 1.9 %collective-permute-start.2 = (f32[16,128]{1,0:T(8,128)S(1)}, f32[16,128]{1,0:T(8,128)S(1)}, u32[]{:S(2)}, u32[]{:S(2)}) collective-permute-start(f32[16,128]{1,0:T(8,128)S(1)} %add.16), channel_id=1, source_target_pairs={{0,4},{1,5},{2,6},{3,7},{4,0},{5,1},{6,2},{7,3},{8,12},{9,13},{10,... | collective-permute-start | bytes 24584 | tf_op jit(solution)/shard_map/ppermute | solution.py:296
  94.5 5.1 %collective-permute-start.1 = (f32[16,128]{1,0:T(8,128)S(1)}, f32[16,128]{1,0:T(8,128)S(1)}, u32[]{:S(2)}, u32[]{:S(2)}) collective-permute-start(f32[16,128]{1,0:T(8,128)S(1)} %add.16), channel_id=1, source_target_pairs={{0,2},{1,3},{2,0},{3,1},{4,6},{5,7},{6,4},{7,5},{8,10},{9,11},{10,... | collective-permute-start | bytes 24584 | tf_op jit(solution)/shard_map/ppermute | solution.py:296
  99.6 0.0 collective-permute-done.3
  99.6 0.0 collective-permute-done.2
  99.6 1.4 %collective-permute-done.1 = f32[16,128]{1,0:T(8,128)S(1)} collective-permute-done((f32[16,128]{1,0:T(8,128)S(1)}, f32[16,128]{1,0:T(8,128)S(1)}, u32[]{:S(2)}, u32[]{:S(2)}) %collective-permute-start.1) | collective-permute-done | bytes 8224 | tf_op jit(solution)/shard_map/ppermute | solution.py:296
  101.0 5.7 %collective-permute-start.6 = (f32[16,128]{1,0:T(8,128)S(1)}, f32[16,128]{1,0:T(8,128)S(1)}, u32[]{:S(2)}, u32[]{:S(2)}) collective-permute-start(f32[16,128]{1,0:T(8,128)S(1)} %add_add_fusion.x_ref), channel_id=1, source_target_pairs={{0,24},{1,25},{2,26},{3,27},{4,28},{5,29},{6,30},{7,31},{8,16},{9,... | collective-permute-start | bytes 24584 | tf_op jit(solution)/shard_map/ppermute | solution.py:296
  106.7 2.6 %collective-permute-start.5 = (f32[16,128]{1,0:T(8,128)S(1)}, f32[16,128]{1,0:T(8,128)S(1)}, u32[]{:S(2)}, u32[]{:S(2)}) collective-permute-start(f32[16,128]{1,0:T(8,128)S(1)} %add_add_fusion.x_ref), channel_id=1, source_target_pairs={{0,16},{1,17},{2,18},{3,19},{4,20},{5,21},{6,22},{7,23},{8,24},{9,... | collective-permute-start | bytes 24584 | tf_op jit(solution)/shard_map/ppermute | solution.py:296
  109.3 3.3 %collective-permute-start.4 = (f32[16,128]{1,0:T(8,128)S(1)}, f32[16,128]{1,0:T(8,128)S(1)}, u32[]{:S(2)}, u32[]{:S(2)}) collective-permute-start(f32[16,128]{1,0:T(8,128)S(1)} %add_add_fusion.x_ref), channel_id=1, source_target_pairs={{0,8},{1,9},{2,10},{3,11},{4,12},{5,13},{6,14},{7,15},{8,0},{9,1},... | collective-permute-start | bytes 24584 | tf_op jit(solution)/shard_map/ppermute | solution.py:296
  112.6 0.0 collective-permute-done.6.three_ref
  112.6 3.5 %collective-permute-done.5.two_ref = f32[16,128]{1,0:T(8,128)S(1)} collective-permute-done((f32[16,128]{1,0:T(8,128)S(1)}, f32[16,128]{1,0:T(8,128)S(1)}, u32[]{:S(2)}, u32[]{:S(2)}) %collective-permute-start.5) | collective-permute-done | bytes 8224 | tf_op jit(solution)/shard_map/ppermute | solution.py:296
  116.1 0.0 collective-permute-done.4.one_ref
  116.1 0.7 gram_copies.1
  116.8 8.1 %all-to-all-done.1 = f32[512,1,768]{2,1,0:T(1,128)S(1)} async-done(((f32[512,1,768]{2,1,0:T(1,128)}), f32[512,1,768]{2,1,0:T(1,128)S(1)}, u32[]{:S(2)}, u32[]{:S(2)}) %all-to-all-start.1) | async-done | bytes 1572896 | tf_op jit(solution)/shard_map/all_to_all | solution.py:273
  125.0 3.5 %all-to-all-start.2 = ((f32[16,1,1536]{2,1,0:T(1,128)}), f32[16,1,1536]{2,1,0:T(1,128)S(1)}, u32[]{:S(2)}, u32[]{:S(2)}) async-start(f32[16,1,1536]{2,1,0:T(1,128)} %bitcast.7), calls=%async_computation.2 | async-start | bytes 196608 | tf_op jit(solution)/shard_map/all_to_all | solution.py:282
  128.5 1.3 turn_back.1
  129.9 6.9 %all-to-all-done.2 = f32[16,1,1536]{2,1,0:T(1,128)S(1)} async-done(((f32[16,1,1536]{2,1,0:T(1,128)}), f32[16,1,1536]{2,1,0:T(1,128)S(1)}, u32[]{:S(2)}, u32[]{:S(2)}) %all-to-all-start.2) | async-done | bytes 98336 | tf_op jit(solution)/shard_map/all_to_all | solution.py:282
  136.8 1.9 %factor.1 = (f32[48,48]{1,0:T(8,128)}, f32[48,48]{1,0:T(8,128)}) custom-call(f32[192,128]{1,0:T(8,128)S(1)} %bitcast.11), custom_call_target="tpu_custom_call" | custom-call | tf_op jit(solution)/shard_map/factor/pallas_call | solution.py:260
  (2 shorter events, 0.0 us)
Async XLA Ops:
  4.1 22.2 %copy-start = (s32[12288]{0:T(1024)S(1)}, s32[12288]{0:T(1024)}, u32[]{:S(2)}) copy-start(s32[12288]{0:T(1024)} %param.5) | copy-start | bytes 147460
  4.1 66.1 %all-to-all-start = ((f32[512,1,768]{2,1,0:T(1,128)}), f32[512,1,768]{2,1,0:T(1,128)S(1)}, u32[]{:S(2)}, u32[]{:S(2)}) async-start(f32[512,1,768]{2,1,0:T(1,128)} %bitcast.1), calls=%async_computation | async-start | bytes 3145728 | tf_op jit(solution)/shard_map/all_to_all | solution.py:273
  72.0 53.0 %all-to-all-start.1 = ((f32[512,1,768]{2,1,0:T(1,128)}), f32[512,1,768]{2,1,0:T(1,128)S(1)}, u32[]{:S(2)}, u32[]{:S(2)}) async-start(f32[512,1,768]{2,1,0:T(1,128)} %bitcast.5), calls=%async_computation.1 | async-start | bytes 3145728 | tf_op jit(solution)/shard_map/all_to_all | solution.py:273
  83.6 7.0 %collective-permute-start = (f32[16,128]{1,0:T(8,128)S(1)}, f32[16,128]{1,0:T(8,128)S(1)}, u32[]{:S(2)}, u32[]{:S(2)}) collective-permute-start(f32[16,128]{1,0:T(8,128)S(1)} %gram_terms.1), channel_id=1, source_target_pairs={{0,1},{1,0},{2,3},{3,2},{4,5},{5,4},{6,7},{7,6},{8,9},{9,8},{10,11... | collective-permute-start | bytes 24584 | tf_op jit(solution)/shard_map/ppermute | solution.py:296
  90.6 9.0 %collective-permute-start.3 = (f32[16,128]{1,0:T(8,128)S(1)}, f32[16,128]{1,0:T(8,128)S(1)}, u32[]{:S(2)}, u32[]{:S(2)}) collective-permute-start(f32[16,128]{1,0:T(8,128)S(1)} %add.16), channel_id=1, source_target_pairs={{0,6},{1,7},{2,4},{3,5},{4,2},{5,3},{6,0},{7,1},{8,14},{9,15},{10,... | collective-permute-start | bytes 24584 | tf_op jit(solution)/shard_map/ppermute | solution.py:296
  92.5 7.1 %collective-permute-start.2 = (f32[16,128]{1,0:T(8,128)S(1)}, f32[16,128]{1,0:T(8,128)S(1)}, u32[]{:S(2)}, u32[]{:S(2)}) collective-permute-start(f32[16,128]{1,0:T(8,128)S(1)} %add.16), channel_id=1, source_target_pairs={{0,4},{1,5},{2,6},{3,7},{4,0},{5,1},{6,2},{7,3},{8,12},{9,13},{10,... | collective-permute-start | bytes 24584 | tf_op jit(solution)/shard_map/ppermute | solution.py:296
  94.5 6.6 %collective-permute-start.1 = (f32[16,128]{1,0:T(8,128)S(1)}, f32[16,128]{1,0:T(8,128)S(1)}, u32[]{:S(2)}, u32[]{:S(2)}) collective-permute-start(f32[16,128]{1,0:T(8,128)S(1)} %add.16), channel_id=1, source_target_pairs={{0,2},{1,3},{2,0},{3,1},{4,6},{5,7},{6,4},{7,5},{8,10},{9,11},{10,... | collective-permute-start | bytes 24584 | tf_op jit(solution)/shard_map/ppermute | solution.py:296
  101.0 11.6 %collective-permute-start.6 = (f32[16,128]{1,0:T(8,128)S(1)}, f32[16,128]{1,0:T(8,128)S(1)}, u32[]{:S(2)}, u32[]{:S(2)}) collective-permute-start(f32[16,128]{1,0:T(8,128)S(1)} %add_add_fusion.x_ref), channel_id=1, source_target_pairs={{0,24},{1,25},{2,26},{3,27},{4,28},{5,29},{6,30},{7,31},{8,16},{9,... | collective-permute-start | bytes 24584 | tf_op jit(solution)/shard_map/ppermute | solution.py:296
  106.7 9.4 %collective-permute-start.5 = (f32[16,128]{1,0:T(8,128)S(1)}, f32[16,128]{1,0:T(8,128)S(1)}, u32[]{:S(2)}, u32[]{:S(2)}) collective-permute-start(f32[16,128]{1,0:T(8,128)S(1)} %add_add_fusion.x_ref), channel_id=1, source_target_pairs={{0,16},{1,17},{2,18},{3,19},{4,20},{5,21},{6,22},{7,23},{8,24},{9,... | collective-permute-start | bytes 24584 | tf_op jit(solution)/shard_map/ppermute | solution.py:296
  109.3 6.8 %collective-permute-start.4 = (f32[16,128]{1,0:T(8,128)S(1)}, f32[16,128]{1,0:T(8,128)S(1)}, u32[]{:S(2)}, u32[]{:S(2)}) collective-permute-start(f32[16,128]{1,0:T(8,128)S(1)} %add_add_fusion.x_ref), channel_id=1, source_target_pairs={{0,8},{1,9},{2,10},{3,11},{4,12},{5,13},{6,14},{7,15},{8,0},{9,1},... | collective-permute-start | bytes 24584 | tf_op jit(solution)/shard_map/ppermute | solution.py:296
  125.0 11.8 %all-to-all-start.2 = ((f32[16,1,1536]{2,1,0:T(1,128)}), f32[16,1,1536]{2,1,0:T(1,128)S(1)}, u32[]{:S(2)}, u32[]{:S(2)}) async-start(f32[16,1,1536]{2,1,0:T(1,128)} %bitcast.7), calls=%async_computation.2 | async-start | bytes 196608 | tf_op jit(solution)/shard_map/all_to_all | solution.py:282

commit v6 on v5

--- a/solution.py
+++ b/solution.py
@@ -41,15 +41,16 @@
     flips_in = pltpu.make_async_copy(flips_ref, signs_ref, flip_sem)
     flips_in.start()
     slab_in = []
-    for tile in range(width // 8):
-        part = pl.ds(tile * 8, 8)
+    for tile in range(width // 16):
+        part = pl.ds(tile * 16, 16)
         slab_in.append(pltpu.make_async_copy(slab_ref.at[part], field_ref.at[part], in_sem.at[tile]))
         slab_in[-1].start()
     flips_in.wait()
     signs = (1 - 2 * signs_ref[...]).astype(jnp.float32) * scale
     for tile in range(width // 8):
         rows8 = pl.ds(tile * 8, 8)
-        slab_in[tile].wait()
+        if tile % 2 == 0:
+            slab_in[tile // 2].wait()
         for first in range(outer // 8):
             parts = []
             for k in range(8):
@@ -317,7 +318,7 @@
             pltpu.VMEM((outer, LANES), jnp.int32),
             pltpu.VMEM((lines, LANES), jnp.float32),
             pltpu.VMEM((lines, LANES), jnp.float32),
-            dma((width // 8,)),
+            dma((width // 16,)),
             dma,
             dma((outer // A_LO,)),
         ],

time: 139 us -> 139 us (level)
  no operation moved by 1% of the time
where the time goes in v6:
time: 139 us
  waiting for transfers between devices  63.4 us (46%)
  starting transfers between devices  61.6 us (44%)
  Pallas kernels  12.9 us (9%)
    all_to_all x2, waiting for transfers between devices, exchange(): lax.all_to_all(x.reshape(blocks, x.size // blocks), AXES, 0, 0, tiled=True)  50.8 us
    all_to_all x2, starting transfers between devices, exchange(): lax.all_to_all(x.reshape(blocks, x.size // blocks), AXES, 0, 0, tiled=True)  31.3 us
    ppermute x7, starting transfers between devices, from_partner(): lax.ppermute(x, AXES, [(i, i ^ apart) for i in range(lax.axis_size(AXES))])  26.7 us
    pallas_call x7, Pallas kernels, call(): pl.pallas_call(kernel, out_shape=out, in_specs=specs or [VMEM] * len(oper...  12.9 us
    all_to_all x1, waiting for transfers between devices, from_all(): lax.all_to_all(parts, AXES, 0, 0, tiled=True, axis_index_groups=groups)  6.91 us
    ppermute x7, waiting for transfers between devices, from_partner(): lax.ppermute(x, AXES, [(i, i ^ apart) for i in range(lax.axis_size(AXES))])  5.7 us
    all_to_all x1, starting transfers between devices, from_all(): lax.all_to_all(parts, AXES, 0, 0, tiled=True, axis_index_groups=groups)  3.51 us
  transfers between devices with their start and end apart: 10, of which 6 were waited for; matrix products, arithmetic and copies ran while one was open for 0% of the time, Pallas kernels for 4%

profile of v6, /device:TPU:1, one launch (start us, length us, event | category | flops | bytes accessed | tf_op | source)
XLA Modules:
  0.0 138.6 jit_solution(4024730632642561738)
XLA Ops:
  0.6 3.5 %local_transform.1 = f32[3072,128]{1,0:T(8,128)} custom-call(f32[48,8192]{1,0:T(8,128)} %refs_0_.1, s32[64,128]{1,0:T(8,128)} %bitcast.13), custom_call_target="tpu_custom_call" | custom-call | tf_op jit(solution)/shard_map/local_transform/pallas_call | solution.py:261
  4.1 0.0 copy-start
  4.1 22.2 %all-to-all-start = ((f32[512,1,768]{2,1,0:T(1,128)}), f32[512,1,768]{2,1,0:T(1,128)S(1)}, u32[]{:S(2)}, u32[]{:S(2)}) async-start(f32[512,1,768]{2,1,0:T(1,128)} %bitcast.1), calls=%async_computation | async-start | bytes 3145728 | tf_op jit(solution)/shard_map/all_to_all | solution.py:274
  26.3 0.0 copy-done
  26.3 1.2 sampled_hits.1.refs_1_
  27.5 42.6 %all-to-all-done = f32[512,1,768]{2,1,0:T(1,128)S(1)} async-done(((f32[512,1,768]{2,1,0:T(1,128)}), f32[512,1,768]{2,1,0:T(1,128)S(1)}, u32[]{:S(2)}, u32[]{:S(2)}) %all-to-all-start) | async-done | bytes 1572896 | tf_op jit(solution)/shard_map/all_to_all | solution.py:274
  70.2 1.8 %block_transform.1.refs_0_ = f32[3072,128]{1,0:T(8,128)} custom-call(f32[3072,128]{1,0:T(8,128)S(1)} %bitcast.10), custom_call_target="tpu_custom_call" | custom-call | tf_op jit(solution)/shard_map/block_transform/pallas_call | solution.py:261
  72.0 9.1 %all-to-all-start.1 = ((f32[512,1,768]{2,1,0:T(1,128)}), f32[512,1,768]{2,1,0:T(1,128)S(1)}, u32[]{:S(2)}, u32[]{:S(2)}) async-start(f32[512,1,768]{2,1,0:T(1,128)} %bitcast.5), calls=%async_computation.1 | async-start | bytes 3145728 | tf_op jit(solution)/shard_map/all_to_all | solution.py:274
  81.1 2.5 %gram_terms.1 = f32[16,128]{1,0:T(8,128)S(1)} custom-call(f32[3072,128]{1,0:T(8,128)} %block_transform.1.refs_0_, f32[64,128]{1,0:T(8,128)S(1)} %sampled_hits.1.refs_1_), custom_call_target="tpu_custom_call" | custom-call | tf_op jit(solution)/shard_map/gram_terms/pallas_call | solution.py:261
  83.6 6.2 %collective-permute-start = (f32[16,128]{1,0:T(8,128)S(1)}, f32[16,128]{1,0:T(8,128)S(1)}, u32[]{:S(2)}, u32[]{:S(2)}) collective-permute-start(f32[16,128]{1,0:T(8,128)S(1)} %gram_terms.1), channel_id=1, source_target_pairs={{0,1},{1,0},{2,3},{3,2},{4,5},{5,4},{6,7},{7,6},{8,9},{9,8},{10,11... | collective-permute-start | bytes 24584 | tf_op jit(solution)/shard_map/ppermute | solution.py:297
  89.8 0.8 collective-permute-done
  90.6 1.9 %collective-permute-start.3 = (f32[16,128]{1,0:T(8,128)S(1)}, f32[16,128]{1,0:T(8,128)S(1)}, u32[]{:S(2)}, u32[]{:S(2)}) collective-permute-start(f32[16,128]{1,0:T(8,128)S(1)} %add.16), channel_id=1, source_target_pairs={{0,6},{1,7},{2,4},{3,5},{4,2},{5,3},{6,0},{7,1},{8,14},{9,15},{10,... | collective-permute-start | bytes 24584 | tf_op jit(solution)/shard_map/ppermute | solution.py:297
  92.5 1.9 %collective-permute-start.2 = (f32[16,128]{1,0:T(8,128)S(1)}, f32[16,128]{1,0:T(8,128)S(1)}, u32[]{:S(2)}, u32[]{:S(2)}) collective-permute-start(f32[16,128]{1,0:T(8,128)S(1)} %add.16), channel_id=1, source_target_pairs={{0,4},{1,5},{2,6},{3,7},{4,0},{5,1},{6,2},{7,3},{8,12},{9,13},{10,... | collective-permute-start | bytes 24584 | tf_op jit(solution)/shard_map/ppermute | solution.py:297
  94.5 5.1 %collective-permute-start.1 = (f32[16,128]{1,0:T(8,128)S(1)}, f32[16,128]{1,0:T(8,128)S(1)}, u32[]{:S(2)}, u32[]{:S(2)}) collective-permute-start(f32[16,128]{1,0:T(8,128)S(1)} %add.16), channel_id=1, source_target_pairs={{0,2},{1,3},{2,0},{3,1},{4,6},{5,7},{6,4},{7,5},{8,10},{9,11},{10,... | collective-permute-start | bytes 24584 | tf_op jit(solution)/shard_map/ppermute | solution.py:297
  99.6 0.0 collective-permute-done.3
  99.6 0.0 collective-permute-done.2
  99.6 1.4 %collective-permute-done.1 = f32[16,128]{1,0:T(8,128)S(1)} collective-permute-done((f32[16,128]{1,0:T(8,128)S(1)}, f32[16,128]{1,0:T(8,128)S(1)}, u32[]{:S(2)}, u32[]{:S(2)}) %collective-permute-start.1) | collective-permute-done | bytes 8224 | tf_op jit(solution)/shard_map/ppermute | solution.py:297
  101.0 5.7 %collective-permute-start.6 = (f32[16,128]{1,0:T(8,128)S(1)}, f32[16,128]{1,0:T(8,128)S(1)}, u32[]{:S(2)}, u32[]{:S(2)}) collective-permute-start(f32[16,128]{1,0:T(8,128)S(1)} %add_add_fusion.x_ref), channel_id=1, source_target_pairs={{0,24},{1,25},{2,26},{3,27},{4,28},{5,29},{6,30},{7,31},{8,16},{9,... | collective-permute-start | bytes 24584 | tf_op jit(solution)/shard_map/ppermute | solution.py:297
  106.7 2.6 %collective-permute-start.5 = (f32[16,128]{1,0:T(8,128)S(1)}, f32[16,128]{1,0:T(8,128)S(1)}, u32[]{:S(2)}, u32[]{:S(2)}) collective-permute-start(f32[16,128]{1,0:T(8,128)S(1)} %add_add_fusion.x_ref), channel_id=1, source_target_pairs={{0,16},{1,17},{2,18},{3,19},{4,20},{5,21},{6,22},{7,23},{8,24},{9,... | collective-permute-start | bytes 24584 | tf_op jit(solution)/shard_map/ppermute | solution.py:297
  109.3 3.3 %collective-permute-start.4 = (f32[16,128]{1,0:T(8,128)S(1)}, f32[16,128]{1,0:T(8,128)S(1)}, u32[]{:S(2)}, u32[]{:S(2)}) collective-permute-start(f32[16,128]{1,0:T(8,128)S(1)} %add_add_fusion.x_ref), channel_id=1, source_target_pairs={{0,8},{1,9},{2,10},{3,11},{4,12},{5,13},{6,14},{7,15},{8,0},{9,1},... | collective-permute-start | bytes 24584 | tf_op jit(solution)/shard_map/ppermute | solution.py:297
  112.6 0.0 collective-permute-done.6.three_ref
  112.6 3.5 %collective-permute-done.5.two_ref = f32[16,128]{1,0:T(8,128)S(1)} collective-permute-done((f32[16,128]{1,0:T(8,128)S(1)}, f32[16,128]{1,0:T(8,128)S(1)}, u32[]{:S(2)}, u32[]{:S(2)}) %collective-permute-start.5) | collective-permute-done | bytes 8224 | tf_op jit(solution)/shard_map/ppermute | solution.py:297
  116.1 0.0 collective-permute-done.4.one_ref
  116.1 0.7 gram_copies.1
  116.8 8.1 %all-to-all-done.1 = f32[512,1,768]{2,1,0:T(1,128)S(1)} async-done(((f32[512,1,768]{2,1,0:T(1,128)}), f32[512,1,768]{2,1,0:T(1,128)S(1)}, u32[]{:S(2)}, u32[]{:S(2)}) %all-to-all-start.1) | async-done | bytes 1572896 | tf_op jit(solution)/shard_map/all_to_all | solution.py:274
  125.0 3.5 %all-to-all-start.2 = ((f32[16,1,1536]{2,1,0:T(1,128)}), f32[16,1,1536]{2,1,0:T(1,128)S(1)}, u32[]{:S(2)}, u32[]{:S(2)}) async-start(f32[16,1,1536]{2,1,0:T(1,128)} %bitcast.7), calls=%async_computation.2 | async-start | bytes 196608 | tf_op jit(solution)/shard_map/all_to_all | solution.py:283
  128.5 1.3 turn_back.1
  129.9 6.9 %all-to-all-done.2 = f32[16,1,1536]{2,1,0:T(1,128)S(1)} async-done(((f32[16,1,1536]{2,1,0:T(1,128)}), f32[16,1,1536]{2,1,0:T(1,128)S(1)}, u32[]{:S(2)}, u32[]{:S(2)}) %all-to-all-start.2) | async-done | bytes 98336 | tf_op jit(solution)/shard_map/all_to_all | solution.py:283
  136.8 1.9 %factor.1 = (f32[48,48]{1,0:T(8,128)}, f32[48,48]{1,0:T(8,128)}) custom-call(f32[192,128]{1,0:T(8,128)S(1)} %bitcast.11), custom_call_target="tpu_custom_call" | custom-call | tf_op jit(solution)/shard_map/factor/pallas_call | solution.py:261
  (2 shorter events, 0.0 us)
Async XLA Ops:
  4.1 22.2 %copy-start = (s32[12288]{0:T(1024)S(1)}, s32[12288]{0:T(1024)}, u32[]{:S(2)}) copy-start(s32[12288]{0:T(1024)} %param.5) | copy-start | bytes 147460
  4.1 66.1 %all-to-all-start = ((f32[512,1,768]{2,1,0:T(1,128)}), f32[512,1,768]{2,1,0:T(1,128)S(1)}, u32[]{:S(2)}, u32[]{:S(2)}) async-start(f32[512,1,768]{2,1,0:T(1,128)} %bitcast.1), calls=%async_computation | async-start | bytes 3145728 | tf_op jit(solution)/shard_map/all_to_all | solution.py:274
  72.0 53.0 %all-to-all-start.1 = ((f32[512,1,768]{2,1,0:T(1,128)}), f32[512,1,768]{2,1,0:T(1,128)S(1)}, u32[]{:S(2)}, u32[]{:S(2)}) async-start(f32[512,1,768]{2,1,0:T(1,128)} %bitcast.5), calls=%async_computation.1 | async-start | bytes 3145728 | tf_op jit(solution)/shard_map/all_to_all | solution.py:274
  83.6 7.0 %collective-permute-start = (f32[16,128]{1,0:T(8,128)S(1)}, f32[16,128]{1,0:T(8,128)S(1)}, u32[]{:S(2)}, u32[]{:S(2)}) collective-permute-start(f32[16,128]{1,0:T(8,128)S(1)} %gram_terms.1), channel_id=1, source_target_pairs={{0,1},{1,0},{2,3},{3,2},{4,5},{5,4},{6,7},{7,6},{8,9},{9,8},{10,11... | collective-permute-start | bytes 24584 | tf_op jit(solution)/shard_map/ppermute | solution.py:297
  90.6 9.0 %collective-permute-start.3 = (f32[16,128]{1,0:T(8,128)S(1)}, f32[16,128]{1,0:T(8,128)S(1)}, u32[]{:S(2)}, u32[]{:S(2)}) collective-permute-start(f32[16,128]{1,0:T(8,128)S(1)} %add.16), channel_id=1, source_target_pairs={{0,6},{1,7},{2,4},{3,5},{4,2},{5,3},{6,0},{7,1},{8,14},{9,15},{10,... | collective-permute-start | bytes 24584 | tf_op jit(solution)/shard_map/ppermute | solution.py:297
  92.5 7.1 %collective-permute-start.2 = (f32[16,128]{1,0:T(8,128)S(1)}, f32[16,128]{1,0:T(8,128)S(1)}, u32[]{:S(2)}, u32[]{:S(2)}) collective-permute-start(f32[16,128]{1,0:T(8,128)S(1)} %add.16), channel_id=1, source_target_pairs={{0,4},{1,5},{2,6},{3,7},{4,0},{5,1},{6,2},{7,3},{8,12},{9,13},{10,... | collective-permute-start | bytes 24584 | tf_op jit(solution)/shard_map/ppermute | solution.py:297
  94.5 6.6 %collective-permute-start.1 = (f32[16,128]{1,0:T(8,128)S(1)}, f32[16,128]{1,0:T(8,128)S(1)}, u32[]{:S(2)}, u32[]{:S(2)}) collective-permute-start(f32[16,128]{1,0:T(8,128)S(1)} %add.16), channel_id=1, source_target_pairs={{0,2},{1,3},{2,0},{3,1},{4,6},{5,7},{6,4},{7,5},{8,10},{9,11},{10,... | collective-permute-start | bytes 24584 | tf_op jit(solution)/shard_map/ppermute | solution.py:297
  101.0 11.6 %collective-permute-start.6 = (f32[16,128]{1,0:T(8,128)S(1)}, f32[16,128]{1,0:T(8,128)S(1)}, u32[]{:S(2)}, u32[]{:S(2)}) collective-permute-start(f32[16,128]{1,0:T(8,128)S(1)} %add_add_fusion.x_ref), channel_id=1, source_target_pairs={{0,24},{1,25},{2,26},{3,27},{4,28},{5,29},{6,30},{7,31},{8,16},{9,... | collective-permute-start | bytes 24584 | tf_op jit(solution)/shard_map/ppermute | solution.py:297
  106.7 9.4 %collective-permute-start.5 = (f32[16,128]{1,0:T(8,128)S(1)}, f32[16,128]{1,0:T(8,128)S(1)}, u32[]{:S(2)}, u32[]{:S(2)}) collective-permute-start(f32[16,128]{1,0:T(8,128)S(1)} %add_add_fusion.x_ref), channel_id=1, source_target_pairs={{0,16},{1,17},{2,18},{3,19},{4,20},{5,21},{6,22},{7,23},{8,24},{9,... | collective-permute-start | bytes 24584 | tf_op jit(solution)/shard_map/ppermute | solution.py:297
  109.3 6.8 %collective-permute-start.4 = (f32[16,128]{1,0:T(8,128)S(1)}, f32[16,128]{1,0:T(8,128)S(1)}, u32[]{:S(2)}, u32[]{:S(2)}) collective-permute-start(f32[16,128]{1,0:T(8,128)S(1)} %add_add_fusion.x_ref), channel_id=1, source_target_pairs={{0,8},{1,9},{2,10},{3,11},{4,12},{5,13},{6,14},{7,15},{8,0},{9,1},... | collective-permute-start | bytes 24584 | tf_op jit(solution)/shard_map/ppermute | solution.py:297
  125.0 11.8 %all-to-all-start.2 = ((f32[16,1,1536]{2,1,0:T(1,128)}), f32[16,1,1536]{2,1,0:T(1,128)S(1)}, u32[]{:S(2)}, u32[]{:S(2)}) async-start(f32[16,1,1536]{2,1,0:T(1,128)} %bitcast.7), calls=%async_computation.2 | async-start | bytes 196608 | tf_op jit(solution)/shard_map/all_to_all | solution.py:283
